TPU v7x, 32 devices: a whole 2x2x4 slice. The times are simulated.
32 devices in a mesh: seq: 4 (over z), exp: 8 (over y, x, core).
Axes of the slice: x: 2, y: 2, z: 4, core: 2. Of those that a mesh axis runs over, the one named last changes fastest.
Arguments:
- layer_input: bfloat16 [8, 2048, 768], P('exp', 'seq'), may hold values from -9 to 9
- lengths: int32 [8, 3], P('exp'), may hold values from 64 to 1792, as said below
- routes: int32 [8, 2048, 2], P('exp', 'seq'), may hold values from 0 to 31, all different within a row
- norm1_gain: float32 [768], replicated, may hold values from 0.5 to 1.5
- qkv_weight: bfloat16 [768, 2304], replicated, may hold values from -0.21875 to 0.21875
- out_weight: bfloat16 [768, 768], replicated, may hold values from -1.25 to 1.25
- norm2_gain: float32 [768], replicated, may hold values from 0.5 to 1.5
- router_weight: bfloat16 [768, 32], replicated, may hold values from -0.15625 to 0.15625
- frozen_up: bfloat16 [16, 768, 3072], P('exp'), may hold values from -0.21875 to 0.21875
- frozen_down: bfloat16 [16, 3072, 768], P('exp'), may hold values from -0.109375 to 0.109375
- train_up: bfloat16 [16, 768, 3072], P('exp'), may hold values from -0.21875 to 0.21875
- train_down: bfloat16 [16, 3072, 768], P('exp'), may hold values from -0.109375 to 0.109375
- cotangent: bfloat16 [8, 2048, 768], P('exp', 'seq'), may hold values from -6 to 6
Outputs:
- output: bfloat16 [8, 2048, 768], P('exp', 'seq')
- input_grad: bfloat16 [8, 2048, 768], P('exp', 'seq')
- norm1_gain_grad: float32 [768], replicated
- qkv_grad: float32 [768, 2304], replicated
- out_grad: float32 [768, 768], replicated
- norm2_gain_grad: float32 [768], replicated
- router_grad: float32 [768, 32], replicated
- train_up_grad: float32 [16, 768, 3072], P('exp')
- train_down_grad: float32 [16, 3072, 768], P('exp')
- stat_roots: float32 [3], replicated
Inputs may be any that keep to these rules, and one draw needn't show every extreme that they name: `lengths`: the 3 documents of a group lie end to end from its first slot, the rest of the group is padding; one document of each group has 1792 tokens, the others at most a quarter of 512.
All inputs are finite; a program needn't handle non-finite values.
Results may differ from a plain program's by a relative error of at most 0.019.
Values may be sent and summed in bfloat16 or wider, within the bound.
No kernel may reach another device: no remote copies, remote signals or barrier semaphores. Data moves between devices by JAX's collectives and lax.ppermute only.
A program may use at most 256 MiB of HBM per device.

v0:
```python
from functools import partial
import math

import jax
import jax.numpy as jnp
from jax import lax
from jax.sharding import PartitionSpec as P

D = 768
HEADS = 12
EXPERTS = 32
FROZEN = 16
CAP = 48


epsilon = 1e-06
masked_score = -1e30


def norm_scaled(values, gain_vector):
    return (
        values
        * lax.rsqrt(jnp.mean(values * values, axis=-1, keepdims=True) + epsilon)
        * gain_vector
    )


def segment_index(positions, doc_bounds):
    return jnp.sum((positions[:, None] >= doc_bounds[None, :]).astype(jnp.int32), axis=1)


def allowed_pairs(query_pos, key_pos, doc_bounds):
    same_doc = (
        segment_index(query_pos, doc_bounds)[:, None] == segment_index(key_pos, doc_bounds)[None, :]
    )
    return same_doc & (key_pos[None, :] <= query_pos[:, None])


def pair_slots(route_rows, valid_rows, expert_count, frozen_count, frozen_dev, capacity):
    flat_routes = route_rows.reshape(-1)
    live_pair = jnp.repeat(valid_rows, 2)
    route_onehot = (
        flat_routes[:, None] == jnp.arange(expert_count, dtype=jnp.int32)[None, :]
    ) & live_pair[:, None]
    running_count = jnp.cumsum(route_onehot.astype(jnp.int32), axis=0)
    place_index = jnp.sum(jnp.where(route_onehot, running_count - 1, 0), axis=1)
    is_frozen = flat_routes < frozen_count
    own_index = jnp.where(is_frozen, flat_routes, flat_routes - frozen_count)
    local_slot = jnp.where(is_frozen, own_index % frozen_dev, frozen_dev + own_index % frozen_dev)
    row_index = own_index // frozen_dev * (2 * frozen_dev) + local_slot
    kept_pair = live_pair & (place_index < capacity)
    slot_index = jnp.where(kept_pair, row_index * capacity + place_index, expert_count * capacity)
    pair_count = flat_routes.shape[0]
    source_pair = (
        jnp.full((expert_count * capacity,), pair_count, jnp.int32)
        .at[slot_index]
        .set(jnp.arange(pair_count, dtype=jnp.int32), mode="drop")
    )
    return (slot_index, source_pair)


def body(
    layer_input,
    lengths,
    routes,
    norm1_gain,
    qkv_weight,
    out_weight,
    norm2_gain,
    router_weight,
    frozen_up,
    frozen_down,
    train_up,
    train_down,
    cotangent,
):
    tok_count = layer_input.shape[1]
    head_width = D // HEADS
    score_scale = head_width ** (-0.5)
    frozen_dev = frozen_up.shape[0]
    expert_dev = 2 * frozen_dev
    exp_groups = lax.axis_size("exp")
    seq_rank = lax.axis_index("seq")
    positions = seq_rank * tok_count + jnp.arange(tok_count, dtype=jnp.int32)
    doc_bounds = jnp.cumsum(lengths[0])
    valid_rows = positions < doc_bounds[-1]
    tokens_in = layer_input[0].astype(jnp.float32)
    normed_one = norm_scaled(tokens_in, norm1_gain).astype(jnp.bfloat16)
    qkv_rows = jnp.dot(normed_one, qkv_weight, preferred_element_type=jnp.float32).astype(
        jnp.bfloat16
    )
    query_flat = qkv_rows[:, :D]
    keys_local = qkv_rows[:, D : 2 * D]
    values_local = qkv_rows[:, 2 * D :]
    queries = query_flat.reshape(tok_count, HEADS, head_width)
    start_state = (
        jnp.full((HEADS, tok_count), masked_score, jnp.float32),
        jnp.zeros((HEADS, tok_count), jnp.float32),
        jnp.zeros((HEADS, tok_count, head_width), jnp.float32),
    )
    key_rows = lax.all_gather(keys_local, "seq", axis=0, tiled=True)
    value_rows = lax.all_gather(values_local, "seq", axis=0, tiled=True)
    row_total = key_rows.shape[0]
    fold_block_width = math.gcd(row_total, 512)
    block_count = row_total // fold_block_width
    key_blocks = key_rows.reshape(block_count, fold_block_width, HEADS, head_width)
    value_blocks = value_rows.reshape(block_count, fold_block_width, HEADS, head_width)
    offsets = jnp.arange(block_count, dtype=jnp.int32) * fold_block_width

    def attend_block(state_now, block_items):
        running_max, running_sum, weighted = state_now
        key_block, value_block, block_start = block_items
        key_pos = block_start + jnp.arange(fold_block_width, dtype=jnp.int32)
        allowed = allowed_pairs(positions, key_pos, doc_bounds)
        scores = (
            jnp.einsum("qhd,khd->hqk", queries, key_block, preferred_element_type=jnp.float32)
            * score_scale
        )
        scores = jnp.where(allowed[None], scores, masked_score)
        new_max = jnp.maximum(running_max, jnp.max(scores, axis=2))
        probs = jnp.where(allowed[None], jnp.exp(scores - new_max[:, :, None]), 0.0)
        decay_factor = jnp.exp(running_max - new_max)
        running_sum = running_sum * decay_factor + jnp.sum(probs, axis=2)
        weighted = weighted * decay_factor[:, :, None] + jnp.einsum(
            "hqk,khd->hqd",
            probs.astype(jnp.bfloat16),
            value_block,
            preferred_element_type=jnp.float32,
        )
        return ((new_max, running_sum, weighted), None)

    result_state, unused_out = lax.scan(
        attend_block, start_state, (key_blocks, value_blocks, offsets)
    )
    running_max, running_sum, weighted = result_state
    attn_heads = (weighted / running_sum[:, :, None]).transpose(1, 0, 2)
    log_sum = running_max + jnp.log(running_sum)
    attn_rounded = attn_heads.reshape(tok_count, D).astype(jnp.bfloat16)
    branch = jnp.dot(attn_rounded, out_weight, preferred_element_type=jnp.float32)
    mid_stream = tokens_in + branch
    normed_two = norm_scaled(mid_stream, norm2_gain).astype(jnp.bfloat16)
    logits = jnp.dot(normed_two, router_weight, preferred_element_type=jnp.float32)
    route_rows = routes[0]
    picked = jnp.take_along_axis(logits, route_rows, axis=1)
    gate_weights = jax.nn.softmax(picked, axis=1)
    slot_index, source_pair = pair_slots(route_rows, valid_rows, EXPERTS, FROZEN, frozen_dev, CAP)
    outgoing = jnp.take(normed_two, source_pair // 2, axis=0, mode="fill", fill_value=0).reshape(
        exp_groups, expert_dev, CAP, D
    )
    up_all = jnp.concatenate([frozen_up, train_up], axis=0)
    down_all = jnp.concatenate([frozen_down, train_down], axis=0)
    arrived = lax.all_to_all(outgoing, "exp", split_axis=0, concat_axis=0, tiled=True)
    hidden_pre = jnp.einsum("seci,eif->secf", arrived, up_all, preferred_element_type=jnp.float32)
    activated = jax.nn.gelu(hidden_pre, approximate=True).astype(jnp.bfloat16)
    result_rows = jnp.einsum(
        "secf,efd->secd", activated, down_all, preferred_element_type=jnp.float32
    ).astype(jnp.bfloat16)
    returned = lax.all_to_all(result_rows, "exp", split_axis=0, concat_axis=0, tiled=True)
    returned, hidden_pre, activated, arrived = (returned, hidden_pre, activated, arrived)
    pair_out = jnp.take(
        returned.reshape(EXPERTS * CAP, D), slot_index, axis=0, mode="fill", fill_value=0
    ).reshape(tok_count, 2, D)
    pair_float = pair_out.astype(jnp.float32)
    expert_mix = jnp.einsum("tk,tkd->td", gate_weights, pair_float)
    output = (mid_stream + expert_mix).astype(jnp.bfloat16)
    out_cot = cotangent[0].astype(jnp.float32)
    pair_grad = (
        (gate_weights[:, :, None] * out_cot[:, None, :])
        .astype(jnp.bfloat16)
        .reshape(2 * tok_count, D)
    )
    gate_grad = jnp.einsum("tkd,td->tk", pair_float, out_cot)
    picked_grad = gate_weights * (
        gate_grad - jnp.sum(gate_weights * gate_grad, axis=1, keepdims=True)
    )
    route_onehot = (
        route_rows[:, :, None] == jnp.arange(EXPERTS, dtype=jnp.int32)[None, None, :]
    ).astype(jnp.float32)
    logit_grad = jnp.einsum("tk,tke->te", picked_grad, route_onehot).astype(jnp.bfloat16)
    router_grad_local = jnp.einsum(
        "td,te->de", normed_two, logit_grad, preferred_element_type=jnp.float32
    )
    normed_grad = jnp.einsum(
        "te,de->td", logit_grad, router_weight, preferred_element_type=jnp.float32
    )
    grad_out_buf = jnp.take(pair_grad, source_pair, axis=0, mode="fill", fill_value=0).reshape(
        exp_groups, expert_dev, CAP, D
    )
    arrived_grad = lax.all_to_all(grad_out_buf, "exp", split_axis=0, concat_axis=0, tiled=True)
    active_grad = jnp.einsum(
        "secd,efd->secf", arrived_grad, down_all, preferred_element_type=jnp.float32
    )
    unused_val, gelu_pull = jax.vjp(partial(jax.nn.gelu, approximate=True), hidden_pre)
    hidden_grad = gelu_pull(active_grad)[0].astype(jnp.bfloat16)
    down_grad_local = jnp.einsum(
        "secf,secd->efd",
        activated[:, frozen_dev:],
        arrived_grad[:, frozen_dev:],
        preferred_element_type=jnp.float32,
    )
    up_grad_local = jnp.einsum(
        "seci,secf->eif",
        arrived[:, frozen_dev:],
        hidden_grad[:, frozen_dev:],
        preferred_element_type=jnp.float32,
    )
    input_terms = jnp.einsum(
        "secf,eif->seci", hidden_grad, up_all, preferred_element_type=jnp.float32
    ).astype(jnp.bfloat16)
    input_back = lax.all_to_all(input_terms, "exp", split_axis=0, concat_axis=0, tiled=True)
    pair_input_grad = jnp.take(
        input_back.reshape(EXPERTS * CAP, D), slot_index, axis=0, mode="fill", fill_value=0
    )
    normed_grad = normed_grad + jnp.sum(
        pair_input_grad.reshape(tok_count, 2, D).astype(jnp.float32), axis=1
    )
    up_total, down_total = (
        lax.psum(up_grad_local.astype(jnp.bfloat16), "seq").astype(jnp.float32),
        lax.psum(down_grad_local.astype(jnp.bfloat16), "seq").astype(jnp.float32),
    )
    unused_two, norm_two_pull = jax.vjp(norm_scaled, mid_stream, norm2_gain)
    stream_part, gain_two_local = norm_two_pull(normed_grad)
    mid_grad = out_cot + stream_part
    branch_grad = mid_grad.astype(jnp.bfloat16)
    out_grad_local = jnp.einsum(
        "td,te->de", attn_rounded, branch_grad, preferred_element_type=jnp.float32
    )
    attn_grad = jnp.einsum(
        "te,de->td", branch_grad, out_weight, preferred_element_type=jnp.float32
    ).astype(jnp.bfloat16)
    attn_grad_heads = attn_grad.reshape(tok_count, HEADS, head_width)
    delta_rows = jnp.sum(attn_grad_heads.astype(jnp.float32) * attn_heads, axis=2).T
    key_all, value_all = (
        lax.all_gather(keys_local, "seq", axis=0, tiled=True),
        lax.all_gather(values_local, "seq", axis=0, tiled=True),
    )
    group_rows = key_all.shape[0]
    block_width = math.gcd(group_rows, 512)
    block_count = group_rows // block_width
    offsets = jnp.arange(block_count, dtype=jnp.int32) * block_width

    def grad_block(query_grad, block_items):
        key_block, value_block, block_start = block_items
        key_pos = block_start + jnp.arange(block_width, dtype=jnp.int32)
        allowed = allowed_pairs(positions, key_pos, doc_bounds)
        scores = (
            jnp.einsum("qhd,khd->hqk", queries, key_block, preferred_element_type=jnp.float32)
            * score_scale
        )
        probs = jnp.where(allowed[None], jnp.exp(scores - log_sum[:, :, None]), 0.0)
        value_grad = jnp.einsum(
            "hqk,qhd->khd",
            probs.astype(jnp.bfloat16),
            attn_grad_heads,
            preferred_element_type=jnp.float32,
        )
        prob_grad = jnp.einsum(
            "qhd,khd->hqk", attn_grad_heads, value_block, preferred_element_type=jnp.float32
        )
        score_grad = (probs * (prob_grad - delta_rows[:, :, None])).astype(jnp.bfloat16)
        query_grad = (
            query_grad
            + jnp.einsum("hqk,khd->qhd", score_grad, key_block, preferred_element_type=jnp.float32)
            * score_scale
        )
        key_grad = (
            jnp.einsum("hqk,qhd->khd", score_grad, queries, preferred_element_type=jnp.float32)
            * score_scale
        )
        return (query_grad, (key_grad, value_grad))

    query_grad, (key_terms, value_terms) = lax.scan(
        grad_block,
        jnp.zeros((tok_count, HEADS, head_width), jnp.float32),
        (
            key_all.reshape(block_count, block_width, HEADS, head_width),
            value_all.reshape(block_count, block_width, HEADS, head_width),
            offsets,
        ),
    )
    key_grad, value_grad = (
        lax.psum_scatter(
            key_terms.reshape(group_rows, D).astype(jnp.bfloat16),
            "seq",
            scatter_dimension=0,
            tiled=True,
        ).astype(jnp.float32),
        lax.psum_scatter(
            value_terms.reshape(group_rows, D).astype(jnp.bfloat16),
            "seq",
            scatter_dimension=0,
            tiled=True,
        ).astype(jnp.float32),
    )
    query_grad = query_grad.reshape(tok_count, D)
    qkv_grad_rows = jnp.concatenate([query_grad, key_grad, value_grad], axis=1).astype(jnp.bfloat16)
    qkv_grad_local = jnp.einsum(
        "td,te->de", normed_one, qkv_grad_rows, preferred_element_type=jnp.float32
    )
    normed_one_grad = jnp.einsum(
        "te,de->td", qkv_grad_rows, qkv_weight, preferred_element_type=jnp.float32
    )
    unused_one, norm_one_pull = jax.vjp(norm_scaled, tokens_in, norm1_gain)
    token_part, gain_one_local = norm_one_pull(normed_one_grad)
    input_grad = (mid_grad + token_part).astype(jnp.bfloat16)
    valid_mask = valid_rows.astype(jnp.float32)[:, None]
    stat_local = jnp.stack(
        [
            jnp.sum(valid_mask * tokens_in * tokens_in),
            jnp.sum(valid_mask * branch * branch),
            jnp.sum(valid_mask * expert_mix * expert_mix),
            jnp.sum(valid_rows.astype(jnp.float32)),
        ]
    )
    qkv_total, out_total, router_total, gain_one_total, gain_two_total, stat_sums = lax.psum(
        (
            qkv_grad_local,
            out_grad_local,
            router_grad_local,
            gain_one_local,
            gain_two_local,
            stat_local,
        ),
        ("seq", "exp"),
    )
    stat_roots = jnp.sqrt(stat_sums[:3] / (stat_sums[3] * D))
    return (
        output[None],
        input_grad[None],
        gain_one_total,
        qkv_total,
        out_total,
        gain_two_total,
        router_total,
        up_total,
        down_total,
        stat_roots,
    )


def solution(mesh):
    return jax.shard_map(
        body,
        mesh=mesh,
        in_specs=(
            P("exp", "seq", None),
            P("exp", None),
            P("exp", "seq", None),
            P(),
            P(),
            P(),
            P(),
            P(),
            P("exp", None, None),
            P("exp", None, None),
            P("exp", None, None),
            P("exp", None, None),
            P("exp", "seq", None),
        ),
        out_specs=(
            P("exp", "seq", None),
            P("exp", "seq", None),
            P(),
            P(),
            P(),
            P(),
            P(),
            P("exp", None, None),
            P("exp", None, None),
            P(),
        ),
        check_vma=False,
    )
```

profile of v0, /device:TPU:0, one launch (start us, length us, event | category | flops | bytes accessed | tf_op | source)
XLA Modules:
  0.0 1557.6 jit_solution(14866159212741408281)
XLA Ops:
  37.2 17.5 %reduce-window.11 = s32[32,8,128]{2,1,0:T(8,128)} reduce-window(s32[32,8,128]{2,1,0:T(8,128)} %fusion.97, s32[]{:T(128)} %constant.163.clone.1), window={size=1x1x128 pad=0_0x0_0x127_0}, to_apply=%region_11.12 | reduce-window | flops 4161536 | bytes 262148 | tf_op jit(solution)/shard_map/reduce-window.1
  63.0 4.7 scatter_custom_fusion
  75.2 5.3 all-gather.5.cloned.1.call-done
  85.2 6.2 reshape.533
  95.7 49.2 %all-gather.3.cloned.1.call-done = bf16[2048,768]{1,0:T(8,128)(2,1)} async-done(((bf16[512,768]{1,0:T(8,128)(2,1)}), bf16[2048,768]{1,0:T(8,128)(2,1)}) %all-gather.3.cloned.1.call-update) | async-done | bytes 3145744 | tf_op jit(solution)/shard_map/all_gather | solution.py:101
  149.5 6.1 reshape.531
  159.9 59.3 %while.30 = (s32[]{:T(128)}, f32[12,512]{1,0:T(8,128)}, f32[12,512]{1,0:T(8,128)}, f32[12,512,64]{1,2,0:T(8,128)}, s32[3]{0:T(128)S(1)}, /*index=5*/s32[4]{0:T(1...) while((s32[]{:T(128)}, f32[12,512]{1,0:T(8,128)}, ...), condition=%wide.region_7.8_spmd.clone, body=%wide.region_2.7_spmd.clone.sunk | while | flops 848206848 | bytes 57594172 | solution.py:132
  168.8 4.7 fusion.182
  198.4 4.7 fusion.182
  227.2 8.1 gather_fusion
  238.6 4.9 all-to-all-start
  247.6 5.3 mul.323
  255.5 8.3 gather_fusion.2
  276.3 8.4 gather_fusion.1
  292.6 18.7 %fusion.55 = f32[4,3072,8,48]{1,3,2,0:T(8,128)} fusion(bf16[2,768,3072]{2,1,0:T(8,128)(2,1)} %param.29, bf16[2,768,3072]{2,1,0:T(8,128)(2,1)} %param.27, bf16[8,4,48,768]{3,2,1,0:T(8,128)(2,1)} %all-to-all-done), kind=kOutput, calls=%fused_computation.83 | convolution fusion | flops 7285506048 | bytes 40108032 | tf_op jit(solution)/shard_map/seci,eif->secf/dot_general | solution.py:153
  311.3 15.8 %convert_bitcast_fusion.1 = bf16[8,4,48,768]{3,2,0,1:T(8,128)(2,1)S(1)} fusion(bf16[2,3072,768]{2,1,0:T(8,128)(2,1)} %param.30, bf16[2,3072,768]{2,1,0:T(8,128)(2,1)} %param.28, f32[4,3072,8,48]{1,3,2,0:T(8,128)} %fusion.55), kind=kOutput, calls=%fused_computation.102 | convolution fusion | flops 7329153024 | bytes 40108032 | tf_op jit(solution)/shard_map/secf,efd->secd/dot_general | solution.py:155
  333.3 22.8 %fusion.49 = bf16[8,4,48,3072]{3,2,0,1:T(8,128)(2,1)} fusion(f32[4,3072,8,48]{1,3,2,0:T(8,128)} %fusion.55, bf16[2,3072,768]{2,1,0:T(8,128)(2,1)} %param.30, bf16[2,3072,768]{2,1,0:T(8,128)(2,1)} %param.28, bf16[8,4,48,768]{3,2,1,0:T(8,128)(2,1)} %all-to-all-done.2), kind=kOutput, calls=%fused_computation.70 | convolution fusion | flops 7379877888 | bytes 49545216 | tf_op jit(solution)/shard_map/secd,efd->secf/dot_general | solution.py:190
  356.2 13.7 convert_bitcast_fusion
  379.0 7.5 gather_fusion.3
  386.5 18.9 %all-to-all-done.3 = bf16[8,4,48,768]{3,2,1,0:T(8,128)(2,1)} async-done(((bf16[8,4,48,768]{3,2,1,0:T(8,128)(2,1)}), bf16[8,4,48,768]{3,2,1,0:T(8,128)(2,1)}, u32[]{:S(2)}, u32[]{:S(2)}) %all-to-all-start.3) | async-done | bytes 2359328 | tf_op jit(solution)/shard_map/all_to_all | solution.py:210
  405.4 7.5 gather_fusion.4
  417.4 5.2 reshape.542
  427.0 4.8 fusion.75
  433.5 6.8 reduce_sum.212
  458.1 122.4 %while.31 = (s32[]{:T(128)}, f32[512,12,64]{0,2,1:T(8,128)}, bf16[4,512,12,64]{1,3,2,0:T(8,128)(2,1)}, bf16[4,512,12,64]{1,3,2,0:T(8,128)(2,1)}, bf16[4,512,12,6...) while((s32[]{:T(128)}, f32[512,12,64]{0,2,1:T(8,128)}, ...), condition=%wide.region_22.24_spmd.clone, body=%wide.region_19.23_spmd.clone.sunk | while | flops 2047091712 | bytes 138711536 | solution.py:272
  459.7 8.1 fusion.193
  467.9 6.1 bitcast_dynamic-update-slice_fusion.5
  474.0 8.4 fusion.194
  490.3 8.1 fusion.193
  498.4 6.1 bitcast_dynamic-update-slice_fusion.5
  504.6 8.4 fusion.194
  520.8 8.1 fusion.193
  529.0 6.1 bitcast_dynamic-update-slice_fusion.5
  535.1 8.4 fusion.194
  551.4 8.1 fusion.193
  559.5 6.1 bitcast_dynamic-update-slice_fusion.5
  565.7 8.4 fusion.194
  594.7 23.8 %bitcast_convert_fusion.1 = bf16[2,768,3072]{2,1,0:T(8,128)(2,1)} fusion(bf16[8,4,48,3072]{3,2,0,1:T(8,128)(2,1)} %fusion.49, bf16[8,4,48,768]{3,2,1,0:T(8,128)(2,1)} %all-to-all-done), kind=kOutput, calls=%fused_computation.74 | convolution fusion | flops 3628597248 | bytes 16515072 | tf_op jit(solution)/shard_map/seci,secf->eif/dot_general | solution.py:201
  618.5 24.0 %bitcast_convert_fusion = bf16[2,3072,768]{2,1,0:T(8,128)(2,1)} fusion(f32[4,3072,8,48]{1,3,2,0:T(8,128)} %fusion.55, bf16[8,4,48,768]{3,2,1,0:T(8,128)(2,1)} %all-to-all-done.2), kind=kOutput, calls=%fused_computation.73 | convolution fusion | flops 3671064576 | bytes 29491200 | tf_op jit(solution)/shard_map/secf,secd->efd/dot_general | solution.py:195
  649.6 57.7 %reduce-scatter.3.cloned.1.call-done = bf16[512,768]{0,1:T(8,128)(2,1)} async-done(((bf16[2048,768]{0,1:T(8,128)(2,1)}), bf16[512,768]{0,1:T(8,128)(2,1)}) %reduce-scatter.3.cloned.1.call-update) | async-done | bytes 786448 | tf_op jit(solution)/shard_map/reduce_scatter | solution.py:282
  707.3 7.1 fusion.80
  715.0 6.9 fusion.64
  724.6 48.9 %all-reduce = (f32[768]{0:T(1024)}, f32[768]{0:T(1024)}, f32[4]{0:T(128)}) all-reduce(f32[768]{0:T(1024)} %get-tuple-element.342, f32[768]{0:T(1024)S(1)} %copy-done.55, f32[4]{0:T(128)S(1)} %pad_maximum_fusion.3), channel_id=1, replica_groups=mesh['seq'=4,'exp'=8] {'seq','exp'}, use_global_device_ids=true, to_apply=%region_27.29 | all-reduce | flops 1540 | bytes 12320 | tf_op jit(solution)/shard_map/psum | solution.py:315
  780.5 561.3 %all-reduce.8.cloned.1.call-done = (bf16[2,768,3072]{2,1,0:T(8,128)(2,1)}, bf16[2,3072,768]{2,1,0:T(8,128)(2,1)}) async-done(((bf16[2,768,3072]{2,1,0:T(8,128)(2,1)}, bf16[2,3072,768]{2,1,0:T(8,128)(2,1)}), (bf16[2,768,3072]{2,1,0:T(8,128)(2,1)}, bf16[2,3072,768]{2,1,0:T(8,128)(2,1)})) %all-reduce.8.cloned.1.call-update) | async-done | bytes 18874384 | tf_op jit(solution)/shard_map/psum | solution.py:218
  1341.9 12.9 convert_element_type.166
  1354.8 12.5 convert_element_type.168
  1367.3 174.6 %all-reduce.6.cloned.1.call-done = (f32[768,2304]{1,0:T(8,128)}, f32[768,768]{1,0:T(8,128)}, f32[768,32]{0,1:T(8,128)}) async-done(((f32[768,2304]{1,0:T(8,128)}, f32[768,768]{1,0:T(8,128)}, f32[768,32]{0,1:T(8,128)}), (f32[768,2304]{1,0:T(8,128)}, f32[768,768]{1,0:T(8,128)}, f32[768,32]{0,1:T(8,128)})) %all-reduce.6.cloned.1.call-update) | async-done | bytes 9535504 | tf_op jit(solution)/shard_map/psum | solution.py:315
  1542.0 6.6 copy.213
  (409 shorter events, 258.7 us)
Async XLA Ops:
  7.2 73.3 %all-gather.5.cloned.1.call-start = ((), (), s32[]{:S(2)}) async-start(), calls=%async_computation.7 | async-start | bytes 3932160 | tf_op jit(solution)/shard_map/all_gather | solution.py:102
  12.7 8.4 copy-start.54
  14.2 130.7 %all-gather.3.cloned.1.call-start = ((), (), s32[]{:S(2)}) async-start(), calls=%async_computation.6 | async-start | bytes 3932160 | tf_op jit(solution)/shard_map/all_gather | solution.py:101
  23.0 40.0 %copy-start.34 = (s32[1024]{0:T(1024)}, s32[1024]{0:T(1024)S(1)}, u32[]{:S(2)}) copy-start(s32[1024]{0:T(1024)S(1)} %eq.75) | copy-start | bytes 12292
  227.2 8.1 copy-start.57
  238.6 49.4 %all-to-all-start = ((bf16[8,4,48,768]{3,2,1,0:T(8,128)(2,1)}), bf16[8,4,48,768]{3,2,1,0:T(8,128)(2,1)}, u32[]{:S(2)}, u32[]{:S(2)}) async-start(bf16[8,4,48,768]{3,2,1,0:T(8,128)(2,1)} %broadcast_select_fusion.1), calls=%async_computation | async-start | bytes 4718592 | tf_op jit(solution)/shard_map/all_to_all | solution.py:152
  255.5 16.7 %copy-start.35 = (s32[1024]{0:T(1024)S(1)}, s32[1024]{0:T(1024)}, u32[]{:S(2)}) copy-start(s32[1024]{0:T(1024)} %copy-done.34) | copy-start | bytes 12292
  265.9 10.4 copy-start.43
  276.2 8.4 copy-start.56
  288.0 40.7 %all-to-all-start.2 = ((bf16[8,4,48,768]{3,2,1,0:T(8,128)(2,1)}), bf16[8,4,48,768]{3,2,1,0:T(8,128)(2,1)}, u32[]{:S(2)}, u32[]{:S(2)}) async-start(bf16[8,4,48,768]{3,2,1,0:T(8,128)(2,1)} %broadcast_select_fusion), calls=%async_computation.2 | async-start | bytes 4718592 | tf_op jit(solution)/shard_map/all_to_all | solution.py:189
  328.7 42.8 %all-to-all-start.1 = ((bf16[8,4,48,768]{3,2,1,0:T(8,128)(2,1)}), bf16[8,4,48,768]{3,2,1,0:T(8,128)(2,1)}, u32[]{:S(2)}, u32[]{:S(2)}) async-start(bf16[8,4,48,768]{3,2,1,0:T(8,128)(2,1)} %copy.139), calls=%async_computation.1 | async-start | bytes 4718592 | tf_op jit(solution)/shard_map/all_to_all | solution.py:158
  371.5 33.9 %all-to-all-start.3 = ((bf16[8,4,48,768]{3,2,1,0:T(8,128)(2,1)}), bf16[8,4,48,768]{3,2,1,0:T(8,128)(2,1)}, u32[]{:S(2)}, u32[]{:S(2)}) async-start(bf16[8,4,48,768]{3,2,1,0:T(8,128)(2,1)} %copy.141), calls=%async_computation.3 | async-start | bytes 4718592 | tf_op jit(solution)/shard_map/all_to_all | solution.py:210
  375.9 273.7 %reduce-scatter.5.cloned.1.call-start = ((), (), s32[]{:S(2)}) async-start(), calls=%async_computation.9 | async-start | bytes 3932160 | tf_op jit(solution)/shard_map/reduce_scatter | solution.py:288
  405.4 7.6 copy-start.66
  451.5 6.5 copy-start.37
  451.5 6.5 copy-start.68
  459.7 8.2 copy-start.17
  459.7 8.2 copy-start.22
  459.7 8.2 copy-start.45
  467.9 6.1 copy-start.42
  474.0 8.4 copy-start.18
  474.0 8.4 copy-start.2
  490.2 8.2 copy-start.17
  490.2 8.2 copy-start.22
  490.3 8.2 copy-start.45
  498.4 6.1 copy-start.42
  504.6 8.4 copy-start.18
  504.6 8.4 copy-start.2
  520.8 8.2 copy-start.17
  520.8 8.2 copy-start.22
  520.8 8.2 copy-start.45
  529.0 6.1 copy-start.42
  535.1 8.4 copy-start.18
  535.1 8.4 copy-start.2
  551.3 8.2 copy-start.17
  551.3 8.2 copy-start.22
  551.3 8.2 copy-start.45
  559.5 6.1 copy-start.42
  565.7 8.4 copy-start.18
  565.7 8.4 copy-start.2
  587.5 119.8 %reduce-scatter.3.cloned.1.call-start = ((), (), s32[]{:S(2)}) async-start(), calls=%async_computation.8 | async-start | bytes 3932160 | tf_op jit(solution)/shard_map/reduce_scatter | solution.py:282
  594.6 747.2 %all-reduce.8.cloned.1.call-start = ((), (), s32[]{:S(2)}) async-start(), calls=%async_computation.11 | async-start | bytes 37748736 | tf_op jit(solution)/shard_map/psum | solution.py:218
  642.5 899.5 %all-reduce.6.cloned.1.call-start = ((), (), s32[]{:S(2)}) async-start(), calls=%async_computation.10 | async-start | bytes 19070976 | tf_op jit(solution)/shard_map/psum | solution.py:315
  645.3 62.0 %copy-start.62 = (f32[512]{0:T(512)S(1)}, f32[512]{0:T(512)}, u32[]{:S(2)}) copy-start(f32[512]{0:T(512)} %copy-done.61) | copy-start | bytes 6148
  645.3 62.0 %copy-start.65 = (f32[768]{0:T(1024)S(1)}, f32[768]{0:T(1024)}, u32[]{:S(2)}) copy-start(f32[768]{0:T(1024)} %param.22) | copy-start | bytes 9220
  715.0 9.6 copy-start.55
  715.0 61.4 %copy-start.51 = (f32[512]{0:T(512)S(1)}, f32[512]{0:T(512)}, u32[]{:S(2)}) copy-start(f32[512]{0:T(512)} %copy-done.50) | copy-start | bytes 6148
  1542.0 6.6 copy-start.23
  (76 other events, 216.7 us)
Sparse Core Ops, SparseCore 0:
  14.3 66.1 all-gather.4
  82.7 62.1 all-gather.2
  587.6 57.1 reduce-scatter.4
  646.9 60.2 reduce-scatter.2
  710.3 631.5 all-reduce.7
  1349.6 192.2 all-reduce.5
where the time goes:
time: 1570 us; the launch traced here: 1560 us
  waiting for transfers between devices  868 us (55%)
  matrix products  299 us (19%)
  local copies, waits for them, and re-layouts  181 us (12%)
  other arithmetic  125 us (8%)
  blocking collectives  48.9 us (3%)
  starting transfers between devices  19.3 us (1%)
    psum x1, waiting for transfers between devices, body(): lax.psum(up_grad_local.astype(jnp.bfloat16), 'seq').astype(jnp.float32)  561 us
    psum x1, waiting for transfers between devices, body(): lax.psum((qkv_grad_local, out_grad_local, router_grad_local, gain_one_loc...  175 us
    reduce_scatter x1, waiting for transfers between devices, body(): lax.psum_scatter(key_terms.reshape(group_rows, D).astype(jnp.bfloat16), '...  57.7 us
    all_gather x1, waiting for transfers between devices, body(): key_rows = lax.all_gather(keys_local, 'seq', axis=0, tiled=True)  49.2 us
    psum x1, blocking collectives, body(): lax.psum((qkv_grad_local, out_grad_local, router_grad_local, gain_one_loc...  48.9 us
    dot_general x4, matrix products, grad_block(): jnp.einsum('qhd,khd->hqk', attn_grad_heads, value_block, preferred_elemen...  33.5 us
    dot_general x4, matrix products, grad_block(): jnp.einsum('qhd,khd->hqk', queries, key_block, preferred_element_type=jnp...  32.6 us
  transfers between devices with their start and end apart: 10, of which 6 were waited for; matrix products, arithmetic and copies ran while one was open for 20% of the time, Pallas kernels for 0%

commit v1 on v0

v1 whole, which is shorter than its diff:
```python
import jax
import jax.numpy as jnp
from jax import lax
from jax.experimental import pallas as pl
from jax.experimental.pallas import tpu as pltpu
from jax.sharding import PartitionSpec as P

D = 768
HEADS = 12
HEAD = 64
EXPERTS = 32
FROZEN = 16
CAP = 48

EPS = 1e-06
MASKED = -1e30
BF = jnp.bfloat16
F32 = jnp.float32
TANH_A = 0.7978845608028654
TANH_B = 0.044715
GRAD_ROWS = 1536
VMEM_BYTES = 56 * 1024 * 1024


def mm(a, b):
    return jnp.dot(a, b, preferred_element_type=F32)


def mm_nt(a, b):
    return lax.dot_general(a, b, (((1,), (1,)), ((), ())), preferred_element_type=F32)


def ein(form, a, b):
    return jnp.einsum(form, a, b, preferred_element_type=F32)


def params():
    return pltpu.CompilerParams(vmem_limit_bytes=VMEM_BYTES)


def gelu_parts(h):
    h2 = h * h
    t = jnp.tanh(h * (TANH_A + (TANH_A * TANH_B) * h2))
    half = 0.5 * t + 0.5
    act = h * half
    slope = half + act * (1.0 - half) * (2.0 * TANH_A + (6.0 * TANH_A * TANH_B) * h2)
    return act, slope


def attend_kernel(
    first, last, where_ref, start_ref, q_ref, k_ref, v_ref, m_in, l_in, acc_in, *rest
):
    if last:
        m_ref, l_ref, acc_ref, out_ref = rest
    else:
        m_ref, l_ref, acc_ref = rest
    block = where_ref[0]
    rows = k_ref.shape[0]
    cols = q_ref.shape[0]

    def work():
        q = q_ref[...]
        k = k_ref[...]
        lane = lax.broadcasted_iota(jnp.int32, q.shape, 1)
        key_pos = block * rows + lax.broadcasted_iota(jnp.int32, (rows, cols), 0)
        allowed = key_pos >= start_ref[...]
        if first:
            query_pos = block * rows + lax.broadcasted_iota(jnp.int32, (rows, cols), 1)
            allowed = allowed & (key_pos <= query_pos)
        for half in range(2):
            mine = (lane < HEAD) if half == 0 else (lane >= HEAD)
            scores = mm_nt(k, jnp.where(mine, q, jnp.zeros_like(q)))
            scores = jnp.where(allowed, scores, MASKED)
            top = jnp.max(scores, axis=0, keepdims=True)
            if not first:
                old = m_in[0, half : half + 1, :]
                top = jnp.maximum(top, old)
            probs = jnp.exp(scores - top)
            total = jnp.sum(probs, axis=0, keepdims=True)
            part = slice(half * HEAD, (half + 1) * HEAD)
            value = mm(v_ref[part, :], probs.astype(BF))
            if not first:
                decay = jnp.exp(old - top)
                total = total + l_in[0, half : half + 1, :] * decay
                value = value + acc_in[part, :] * decay
            m_ref[0, half : half + 1, :] = top
            l_ref[0, half : half + 1, :] = total
            acc_ref[part, :] = value

    if first:
        work()
    else:

        @pl.when(block >= 0)
        def _():
            work()

        @pl.when(block < 0)
        def _():
            m_ref[...] = m_in[...]
            l_ref[...] = l_in[...]
            acc_ref[...] = acc_in[...]

    if last:
        for half in range(2):
            part = slice(half * HEAD, (half + 1) * HEAD)
            total = l_ref[0, half : half + 1, :]
            acc_ref[part, :] = acc_ref[part, :] / total
            l_ref[0, half : half + 1, :] = m_ref[0, half : half + 1, :] + jnp.log(total)
        out_ref[...] = acc_ref[...].T.astype(BF)


def attend_step(step, last, block, start, q, k, v_t, state):
    tok = q.shape[0]
    pairs = HEADS // 2
    first = step == 0
    stat = jax.ShapeDtypeStruct((pairs, 2, tok), F32)
    acc = jax.ShapeDtypeStruct((D, tok), F32)
    if first:
        state = (jnp.zeros(stat.shape, F32), jnp.zeros(stat.shape, F32), jnp.zeros(acc.shape, F32))
    outs = [stat, stat, acc] + ([jax.ShapeDtypeStruct((tok, D), BF)] if last else [])
    stat_spec = pl.BlockSpec((1, 2, tok), lambda p, w: (p, 0, 0))
    acc_spec = pl.BlockSpec((2 * HEAD, tok), lambda p, w: (p, 0))
    row_spec = pl.BlockSpec((tok, 2 * HEAD), lambda p, w: (0, p))
    out_specs = [stat_spec, stat_spec, acc_spec] + ([row_spec] if last else [])

    def kernel(*refs):
        attend_kernel(first, last, *refs)

    return pl.pallas_call(
        kernel,
        out_shape=outs,
        grid_spec=pltpu.PrefetchScalarGridSpec(
            num_scalar_prefetch=1,
            grid=(pairs,),
            in_specs=[
                pl.BlockSpec((1, tok), lambda p, w: (0, 0)),
                row_spec,
                row_spec,
                acc_spec,
                stat_spec,
                stat_spec,
                acc_spec,
            ],
            out_specs=out_specs,
        ),
        compiler_params=params(),
        cost_estimate=pl.CostEstimate(
            flops=4 * tok * tok * D, bytes_accessed=8 * tok * D, transcendentals=tok * tok * HEADS
        ),
        name="attend_step",
    )(block, start, q, k, v_t, *state)


def attend_back_kernel(
    blocks, start_ref, q_ref, k_ref, v_ref, do_ref, lse_ref, delta_ref, out_ref, dq_ref, k_t_ref
):
    head = pl.program_id(0)
    rows = q_ref.shape[0] // blocks
    lane = lax.broadcasted_iota(jnp.int32, (rows, 2 * HEAD), 1)
    mine = (lane // HEAD) == lax.rem(head, 2)
    low = lax.rem(head, 2) == 0
    dq_ref[...] = jnp.zeros_like(dq_ref)

    def pick(x):
        return jnp.where(low, x[:HEAD, :], x[HEAD:, :])

    def key_step(kb, carry):
        key_rows = pl.ds(pl.multiple_of(kb * rows, rows), rows)
        k = k_ref[key_rows, :]
        zero = jnp.zeros_like(k)
        k_mine = jnp.where(mine, k, zero)
        v_mine = jnp.where(mine, v_ref[key_rows, :], zero)
        k_t_ref[...] = pick(k.T)

        def pair(qb, diagonal, dk, dv):
            query_rows = pl.ds(pl.multiple_of(qb * rows, rows), rows)
            q = q_ref[query_rows, :]
            do = do_ref[query_rows, :]
            key_pos = kb * rows + lax.broadcasted_iota(jnp.int32, (rows, rows), 0)
            allowed = key_pos >= start_ref[qb]
            if diagonal:
                query_pos = kb * rows + lax.broadcasted_iota(jnp.int32, (rows, rows), 1)
                allowed = allowed & (key_pos <= query_pos)
            scores = mm_nt(k_mine, q)
            probs = jnp.where(allowed, jnp.exp(scores - lse_ref[qb, 0]), 0.0)
            dprobs = mm_nt(v_mine, do)
            dscores = (probs * (dprobs - delta_ref[qb, 0])).astype(BF)
            dv = dv + mm(probs.astype(BF), do)
            dk = dk + mm(dscores, q)
            dq_ref[qb] = dq_ref[qb] + mm(k_t_ref[...], dscores)
            return dk, dv

        empty = jnp.zeros((rows, 2 * HEAD), F32)
        dk, dv = pair(kb, True, empty, empty)
        dk, dv = lax.fori_loop(kb + 1, blocks, lambda qb, c: pair(qb, False, *c), (dk, dv))
        out_ref[kb, 1] = pick(dk.T).astype(BF)
        out_ref[kb, 2] = pick(dv.T).astype(BF)
        return carry

    lax.fori_loop(0, blocks, key_step, 0)
    for b in range(blocks):
        out_ref[b, 0] = (dq_ref[b] * HEAD**-0.5).astype(BF)


def attend_back(blocks, heads, start, qkv, do, lse, delta):
    rows = qkv.shape[0]
    tok = rows // blocks
    slabs = qkv.shape[1] // (3 * 2 * HEAD)

    def part(i):
        return pl.BlockSpec((rows, 2 * HEAD), lambda h: (0, i * slabs + h // 2))

    stat_spec = pl.BlockSpec((blocks, 1, 1, tok), lambda h: (0, h, 0, 0))

    def kernel(*refs):
        attend_back_kernel(blocks, *refs)

    return pl.pallas_call(
        kernel,
        out_shape=jax.ShapeDtypeStruct((blocks, 3, heads * HEAD, tok), BF),
        grid=(heads,),
        in_specs=[
            pl.BlockSpec((blocks, 1, tok), lambda h: (0, 0, 0)),
            part(0),
            part(1),
            part(2),
            part(0),
            stat_spec,
            stat_spec,
        ],
        out_specs=pl.BlockSpec((blocks, 3, HEAD, tok), lambda h: (0, 0, h, 0)),
        scratch_shapes=[pltpu.VMEM((blocks, HEAD, tok), F32), pltpu.VMEM((HEAD, tok), BF)],
        compiler_params=params(),
        cost_estimate=pl.CostEstimate(
            flops=5 * rows * rows * heads * HEAD,
            bytes_accessed=16 * rows * heads * HEAD,
            transcendentals=rows * rows * heads // 2,
        ),
        name="attend_back",
    )(start, qkv, qkv, qkv, do, lse, delta)


def expert_kernel(
    x_ref, g_ref, gate_ref, up_ref, down_ref, mix_ref, dx_ref, dgate_ref, xs, dos, eacc, dacc
):
    step = pl.program_id(1)
    rows = xs.shape[0]
    block = x_ref.shape

    @pl.when(step == 0)
    def _():
        xs[...] = x_ref[...].reshape(rows, D)
        dos[...] = (gate_ref[0] * g_ref[...].reshape(rows, D).astype(F32)).astype(BF)
        eacc[...] = jnp.zeros_like(eacc)
        dacc[...] = jnp.zeros_like(dacc)

    act, slope = gelu_parts(mm(xs[...], up_ref[0]))
    dhid = (mm_nt(dos[...], down_ref[0]) * slope).astype(BF)
    eacc[...] += mm(act.astype(BF), down_ref[0])
    dacc[...] += mm_nt(dhid, up_ref[0])

    @pl.when(step == pl.num_programs(1) - 1)
    def _():
        out = eacc[...]
        g = g_ref[...].reshape(rows, D).astype(F32)
        mix_ref[...] = (gate_ref[0] * out).astype(BF).reshape(block)
        dx_ref[...] = dacc[...].astype(BF).reshape(block)
        dgate_ref[0] = jnp.sum(g * out, axis=1, keepdims=True)


def expert_rows(x, g, gate, up, down):
    sources, experts = x.shape[:2]
    rows = sources * CAP
    hidden = up.shape[2]
    tile = 768
    row_spec = pl.BlockSpec((sources, 1, CAP, D), lambda e, f: (0, e, 0, 0))
    gate_spec = pl.BlockSpec((1, rows, 1), lambda e, f: (e, 0, 0))
    return pl.pallas_call(
        expert_kernel,
        out_shape=[
            jax.ShapeDtypeStruct(x.shape, BF),
            jax.ShapeDtypeStruct(x.shape, BF),
            jax.ShapeDtypeStruct((experts, rows, 1), F32),
        ],
        grid=(experts, hidden // tile),
        in_specs=[
            row_spec,
            row_spec,
            gate_spec,
            pl.BlockSpec((1, D, tile), lambda e, f: (e, 0, f)),
            pl.BlockSpec((1, tile, D), lambda e, f: (e, f, 0)),
        ],
        out_specs=[row_spec, row_spec, gate_spec],
        scratch_shapes=[
            pltpu.VMEM((rows, D), BF),
            pltpu.VMEM((rows, D), BF),
            pltpu.VMEM((rows, D), F32),
            pltpu.VMEM((rows, D), F32),
        ],
        compiler_params=params(),
        cost_estimate=pl.CostEstimate(
            flops=8 * experts * rows * D * hidden,
            bytes_accessed=4 * experts * D * hidden,
            transcendentals=experts * rows * hidden,
        ),
        name="expert_rows",
    )(x, g, gate, up, down)


def expert_grad_kernel(blocks, gate_ref, up_ref, down_ref, *refs):
    x_refs, g_refs = refs[:blocks], refs[blocks : 2 * blocks]
    dup_ref, ddown_ref, xs, dos, xs_t = refs[2 * blocks :]
    rows = xs.shape[0] // blocks

    @pl.when(pl.program_id(1) == 0)
    def _():
        for b in range(blocks):
            part = slice(b * rows, (b + 1) * rows)
            x = x_refs[b][...].reshape(rows, D)
            xs[part, :] = x
            xs_t[:, part] = x.T
            g = g_refs[b][...].reshape(rows, D).astype(F32)
            dos[part, :] = (gate_ref[0, part, :] * g).astype(BF)

    hid = mm_nt(up_ref[0].T, xs[...])
    act, slope = gelu_parts(hid)
    dhid = (mm_nt(down_ref[0], dos[...]) * slope).astype(BF)
    ddown_ref[0] = mm(act.astype(BF), dos[...])
    dup_ref[0] = mm_nt(xs_t[...], dhid)


def expert_grads(xs, gs, gate, up, down):
    blocks = len(xs)
    sources, experts = xs[0].shape[:2]
    rows = blocks * sources * CAP
    hidden = up.shape[2]
    tile = 512
    row_spec = pl.BlockSpec((sources, 1, CAP, D), lambda e, f: (0, e, 0, 0))
    up_spec = pl.BlockSpec((1, D, tile), lambda e, f: (e, 0, f))
    down_spec = pl.BlockSpec((1, tile, D), lambda e, f: (e, f, 0))

    def kernel(*refs):
        expert_grad_kernel(blocks, *refs)

    return pl.pallas_call(
        kernel,
        out_shape=[
            jax.ShapeDtypeStruct(up.shape, F32),
            jax.ShapeDtypeStruct(down.shape, F32),
        ],
        grid=(experts, hidden // tile),
        in_specs=[pl.BlockSpec((1, rows, 1), lambda e, f: (e, 0, 0)), up_spec, down_spec]
        + [row_spec] * (2 * blocks),
        out_specs=[up_spec, down_spec],
        scratch_shapes=[
            pltpu.VMEM((rows, D), BF),
            pltpu.VMEM((rows, D), BF),
            pltpu.VMEM((D, rows), BF),
        ],
        compiler_params=params(),
        cost_estimate=pl.CostEstimate(
            flops=8 * experts * rows * D * hidden,
            bytes_accessed=12 * experts * D * hidden,
            transcendentals=experts * rows * hidden,
        ),
        name="expert_grads",
    )(gate, up, down, *xs, *gs)


def expert_grads_all(xs, gs, gates, up, down):
    group = max(1, GRAD_ROWS // gates[0].shape[1])
    totals = None
    for first in range(0, len(xs), group):
        part = slice(first, first + group)
        gate = jnp.concatenate(gates[part], axis=1)
        grads = expert_grads(xs[part], gs[part], gate, up, down)
        totals = grads if totals is None else [t + g for t, g in zip(totals, grads)]
    return totals


def unit_rows(values):
    return values * lax.rsqrt(jnp.mean(values * values, axis=-1, keepdims=True) + EPS)


def unit_back(values, gain, grad):
    r = lax.rsqrt(jnp.mean(values * values, axis=-1, keepdims=True) + EPS)
    u = values * r
    scaled = grad * gain
    return r * (scaled - u * jnp.mean(scaled * u, axis=-1, keepdims=True)), u


def ring_next(x, count):
    return lax.ppermute(x, "seq", [(i, (i + 1) % count) for i in range(count)])


def ring_all(x, count):
    found = [x]
    for _ in range(count - 1):
        found.append(ring_next(found[-1], count))
    return found


def swap(x, axis):
    return lax.all_to_all(x, axis, split_axis=0, concat_axis=0, tiled=True)


def after(x, *others):
    return lax.optimization_barrier((x,) + others)[0]


def body(
    layer_input,
    lengths,
    routes,
    norm1_gain,
    qkv_weight,
    out_weight,
    norm2_gain,
    router_weight,
    frozen_up,
    frozen_down,
    train_up,
    train_down,
    cotangent,
):
    tok = layer_input.shape[1]
    n_seq = lax.axis_size("seq")
    n_exp = lax.axis_size("exp")
    rank = lax.axis_index("seq")
    heads = -(-HEADS // n_seq)
    slots = heads + heads % 2
    x_own = layer_input[0]
    g_own = cotangent[0]
    bounds = jnp.cumsum(lengths[0])

    scale = HEAD**-0.5
    w_q = qkv_weight[:, :D] * jnp.asarray(scale, BF)
    w_k = qkv_weight[:, D : 2 * D]
    w_v = qkv_weight[:, 2 * D :]
    w_parts = jnp.pad(
        qkv_weight.reshape(D, 3, HEADS, HEAD), ((0, 0), (0, 0), (0, heads * n_seq - HEADS), (0, 0))
    )
    w_groups = w_parts.reshape(D, 3, n_seq, heads * HEAD)
    w_by_group = w_groups.transpose(0, 2, 1, 3).reshape(D, n_seq * 3 * heads * HEAD)
    w_mine = lax.dynamic_index_in_dim(w_groups, rank, axis=2, keepdims=False)
    w_mine = w_mine * jnp.asarray([scale, 1.0, 1.0], BF)[None, :, None]
    w_mine = jnp.pad(w_mine, ((0, 0), (0, 0), (0, (slots - heads) * HEAD)))
    w_mine = w_mine.reshape(D, 3 * slots * HEAD)

    pos_all = jnp.arange(n_seq * tok, dtype=jnp.int32)
    start_all = jnp.max(jnp.where(pos_all[None, :] >= bounds[:, None], bounds[:, None], 0), axis=0)
    pos_own = rank * tok + jnp.arange(tok, dtype=jnp.int32)
    start_own = jnp.max(jnp.where(pos_own[None, :] >= bounds[:, None], bounds[:, None], 0), axis=0)
    valid = pos_own < bounds[-1]
    expert_ids = jnp.arange(EXPERTS, dtype=jnp.int32)[:, None]
    route_rows = routes[0]
    routed = (expert_ids == route_rows[:, 0][None, :]) | (expert_ids == route_rows[:, 1][None, :])
    live = routed & valid[None, :]
    order = jnp.arange(tok, dtype=jnp.int32)
    earlier = (order[:, None] < order[None, :]).astype(BF)
    place = mm(live.astype(BF), earlier).astype(jnp.int32)
    taken = (
        live[:, None, :]
        & (place[:, None, :] == jnp.arange(CAP, dtype=jnp.int32)[None, :, None])
    )
    pick = taken.astype(BF)

    def halves(rows):
        return [
            rows[i * FROZEN : (i + 1) * FROZEN].reshape((n_exp, FROZEN // n_exp) + rows.shape[1:])
            for i in range(2)
        ]

    def project(x):
        n1 = (unit_rows(x.astype(F32)) * norm1_gain).astype(BF)
        return n1, mm(n1, w_k).astype(BF), ein("de,td->et", w_v, n1).astype(BF)

    n1_own, k_own, v_own = project(x_own)
    q_own = mm(n1_own, w_q).astype(BF)
    n1_all = jnp.zeros((n_seq * tok, D), BF)
    x_now = x_own
    state = None
    for step in range(n_seq):
        if step == 0:
            n1, k, v_t = n1_own, k_own, v_own
        else:
            x_now = ring_next(x_now, n_seq)
            n1, k, v_t = project(x_now)
        n1_all = lax.dynamic_update_slice(n1_all, n1, (lax.rem(rank - step + n_seq, n_seq) * tok, 0))
        block = jnp.reshape(rank - step, (1,)).astype(jnp.int32)
        state = attend_step(
            step, step == n_seq - 1, block, start_own[None, :], q_own, k, v_t, state
        )
    unused, lse, attn_t, attn = state

    g_frozen, g_train = [swap(h, "exp") for h in halves(ein("ect,td->ecd", pick, g_own).astype(BF))]

    tokens_in = x_own.astype(F32)
    branch = mm(attn, out_weight)
    mid = tokens_in + branch
    n2 = (unit_rows(mid) * norm2_gain).astype(BF)
    logits = ein("de,td->et", router_weight, n2)
    gates = jax.nn.softmax(jnp.where(routed, logits, -jnp.inf), axis=0)
    slot_gate = jnp.sum(jnp.where(taken, gates[:, None, :], 0.0), axis=2)
    sent = ein("ect,td->ecd", pick, n2).astype(BF)
    x_frozen, x_train = [swap(h, "exp") for h in halves(sent)]
    gate_frozen, gate_train = [swap(h, "exp") for h in halves(slot_gate)]

    def by_expert(gate):
        return gate.transpose(1, 0, 2).reshape(gate.shape[1], -1, 1)

    mix_t, dx_t, dgate_t = expert_rows(x_train, g_train, by_expert(gate_train), train_up, train_down)
    mix_f, dx_f, dgate_f = expert_rows(
        x_frozen, g_frozen, by_expert(gate_frozen), frozen_up, frozen_down
    )

    def from_expert(dgate):
        return dgate.reshape(-1, n_exp, CAP).transpose(1, 0, 2)

    def joined(frozen_part, train_part):
        parts = [swap(frozen_part, "exp"), swap(train_part, "exp")]
        return jnp.concatenate([p.reshape((FROZEN,) + p.shape[2:]) for p in parts], axis=0)

    dx_rows = joined(dx_f, dx_t)
    dgate_slots = joined(from_expert(dgate_f), from_expert(dgate_t))
    mix_rows = joined(mix_f, mix_t)

    xs = ring_all(x_train, n_seq)
    gs = ring_all(g_train, n_seq)
    gate_blocks = [by_expert(p) for p in ring_all(gate_train, n_seq)]

    expert_mix = ein("ect,ecd->td", pick, mix_rows)
    output = (mid + expert_mix).astype(BF)
    dgates = jnp.sum(jnp.where(taken, dgate_slots[:, :, None], 0.0), axis=1)
    dlogits = (gates * (dgates - jnp.sum(gates * dgates, axis=0, keepdims=True))).astype(BF)
    router_part = ein("td,et->de", n2, dlogits)
    dn2 = ein("et,de->td", dlogits, router_weight) + ein("ect,ecd->td", pick, dx_rows)
    dx_mid, u2 = unit_back(mid, norm2_gain, dn2)
    gain2_part = jnp.sum(dn2 * u2, axis=0)
    dmid = g_own.astype(F32) + dx_mid
    dbranch = dmid.astype(BF)
    out_part = ein("td,te->de", attn, dbranch)

    out_groups = jnp.pad(out_weight, ((0, heads * n_seq * HEAD - D), (0, 0)))
    dattn = ein("te,gde->gtd", dbranch, out_groups.reshape(n_seq, heads * HEAD, D)).astype(BF)
    dattn_t = ein("de,te->dt", out_weight, dbranch)
    delta = jnp.sum((dattn_t.astype(BF).astype(F32) * attn_t).reshape(HEADS, HEAD, tok), axis=1)

    def stat_groups(stat):
        stat = jnp.pad(stat.reshape(HEADS, tok), ((0, heads * n_seq - HEADS), (0, 0)))
        return stat.reshape(n_seq, heads, 1, tok)

    do = swap(dattn, "seq").reshape(n_seq * tok, heads * HEAD)
    do = jnp.pad(do, ((0, 0), (0, (slots - heads) * HEAD)))
    stats = swap(jnp.stack([stat_groups(lse), stat_groups(delta)], axis=1), "seq")
    qkv_mine = mm(n1_all, w_mine).astype(BF)
    dqkv_t = attend_back(
        n_seq, heads, start_all.reshape(n_seq, 1, tok), qkv_mine, do, stats[:, 0], stats[:, 1]
    )
    dqkv_t = dqkv_t.reshape(n_seq, 3 * heads * HEAD, tok)
    qkv_part = ein("ntd,nct->dc", n1_all.reshape(n_seq, tok, D), dqkv_t)
    dqkv_own = swap(dqkv_t, "seq").reshape(n_seq * 3 * heads * HEAD, tok)

    pieces = swap(qkv_part.astype(BF).reshape(n_exp, D // n_exp, 3 * heads * HEAD), "exp")
    piece = jnp.sum(pieces.astype(F32), axis=0).astype(BF)
    whole = lax.all_gather(piece, ("seq", "exp"), axis=0, tiled=False)
    whole = whole.reshape(n_seq, D, 3, heads * HEAD).transpose(1, 2, 0, 3)
    qkv_total = whole.reshape(D, 3, n_seq * heads * HEAD)[:, :, :D].reshape(D, 3 * D).astype(F32)
    gain1_total = jnp.sum(qkv_total * qkv_weight.astype(F32), axis=1) / norm1_gain

    up_total, down_total = expert_grads_all(xs, gs, gate_blocks, train_up, train_down)

    dn1 = ein("dc,ct->td", w_by_group, dqkv_own)
    dx_in, unused_u = unit_back(tokens_in, norm1_gain, dn1)
    input_grad = (dmid + dx_in).astype(BF)

    mask = valid.astype(F32)[:, None]
    stat_part = jnp.stack(
        [
            jnp.sum(mask * tokens_in * tokens_in),
            jnp.sum(mask * branch * branch),
            jnp.sum(mask * expert_mix * expert_mix),
            jnp.sum(mask),
        ]
    )
    out_total, router_total = lax.psum(
        (out_part.astype(BF), router_part.astype(BF)), ("seq", "exp")
    )
    gain2_total, stat_sums = lax.psum((gain2_part, stat_part), ("seq", "exp"))
    stat_roots = jnp.sqrt(stat_sums[:3] / (stat_sums[3] * D))
    return (
        output[None],
        input_grad[None],
        gain1_total,
        qkv_total,
        out_total.astype(F32),
        gain2_total,
        router_total.astype(F32),
        up_total,
        down_total,
        stat_roots,
    )


def solution(mesh):
    return jax.shard_map(
        body,
        mesh=mesh,
        in_specs=(
            P("exp", "seq", None),
            P("exp", None),
            P("exp", "seq", None),
            P(),
            P(),
            P(),
            P(),
            P(),
            P("exp", None, None),
            P("exp", None, None),
            P("exp", None, None),
            P("exp", None, None),
            P("exp", "seq", None),
        ),
        out_specs=(
            P("exp", "seq", None),
            P("exp", "seq", None),
            P(),
            P(),
            P(),
            P(),
            P(),
            P("exp", None, None),
            P("exp", None, None),
            P(),
        ),
        check_vma=False,
    )
```

time: 1570 us -> 745 us (0.47)
  waiting for transfers between devices: 868 us -> 185 us
  matrix products: 299 us -> 63.7 us
  Pallas kernels: 0 us -> 173 us
  local copies, waits for them, and re-layouts: 181 us -> 76.4 us
  other arithmetic: 125 us -> 39.7 us
  blocking collectives: 48.9 us -> 110 us
  starting transfers between devices: 19.3 us -> 70.4 us
    psum x2 -> x1, waiting for transfers between devices: 736 us -> 3.81 us  [body(): lax.psum((out_part.astype(BF), router_part.astype(BF)), ('seq', 'exp'))]
    dot_general x46 -> x24, matrix products: 299 us -> 63.7 us  [the longest x16 43 us: ein(): return jnp.einsum(form, a, b, preferred_element_type=F32)]
    pallas_call x0 -> x8, Pallas kernels: none -> 173 us  [the longest x1 71.8 us: expert_grads(): pl.pallas_call(kernel, out_shape=[jax.ShapeDtypeStruct(up.shape, F32), ja...]
    all_to_all x4 -> x14, waiting for transfers between devices: 18.9 us -> 105 us  [swap(): return lax.all_to_all(x, axis, split_axis=0, concat_axis=0, tiled=True)]
    ppermute x0 -> x12, waiting for transfers between devices: none -> 70.1 us  [ring_next(): return lax.ppermute(x, 'seq', [(i, (i + 1) % count) for i in range(count)])]
    reduce_scatter x2 -> x0, waiting for transfers between devices: 57.7 us -> none  [the longest x1 57.7 us: body(): lax.psum_scatter(key_terms.reshape(group_rows, D).astype(jnp.bfloat16), '...]
    all_gather x2 -> x1, waiting for transfers between devices: 54.5 us -> 7.05 us  [body(): whole = lax.all_gather(piece, ('seq', 'exp'), axis=0, tiled=False)]
    gather x8 -> x0, local copies, waits for them, and re-layouts: 43.4 us -> none  [the longest x4 11.8 us: body(): picked = jnp.take_along_axis(logits, route_rows, axis=1)]
  transfers between devices with their start and end apart: 10 -> 28, of which waited for: 6 -> 16; matrix products, arithmetic and copies ran while one was open for 20% -> 20% of each run, Pallas kernels for 0% -> 24%
where the time goes in v1:
time: 745 us; the launch traced here: 735 us
  waiting for transfers between devices  185 us (25%)
  Pallas kernels  173 us (23%)
  blocking collectives  110 us (15%)
  local copies, waits for them, and re-layouts  76.4 us (10%)
  starting transfers between devices  70.4 us (9%)
  matrix products  63.7 us (9%)
  other arithmetic  39.7 us (5%)
  between operations  15.8 us (2%)
    all_to_all x14, waiting for transfers between devices, swap(): return lax.all_to_all(x, axis, split_axis=0, concat_axis=0, tiled=True)  105 us
    pallas_call x1, Pallas kernels, expert_grads(): pl.pallas_call(kernel, out_shape=[jax.ShapeDtypeStruct(up.shape, F32), ja...  71.8 us
    ppermute x12, waiting for transfers between devices, ring_next(): return lax.ppermute(x, 'seq', [(i, (i + 1) % count) for i in range(count)])  70.1 us
    all_to_all x14, starting transfers between devices, swap(): return lax.all_to_all(x, axis, split_axis=0, concat_axis=0, tiled=True)  61.1 us
    dot_general x16, matrix products, ein(): return jnp.einsum(form, a, b, preferred_element_type=F32)  43 us
    pallas_call x2, Pallas kernels, expert_rows(): pl.pallas_call(expert_kernel, out_shape=[jax.ShapeDtypeStruct(x.shape, BF...  42.7 us
    psum x1, blocking collectives, body(): gain2_total, stat_sums = lax.psum((gain2_part, stat_part), ('seq', 'exp'))  40.7 us
    psum x1, blocking collectives, body(): lax.psum((out_part.astype(BF), router_part.astype(BF)), ('seq', 'exp'))  39.8 us
  transfers between devices with their start and end apart: 28, of which 16 were waited for; matrix products, arithmetic and copies ran while one was open for 20% of the time, Pallas kernels for 24%

profile of v1, /device:TPU:0, one launch (start us, length us, event | category | flops | bytes accessed | tf_op | source)
XLA Modules:
  0.0 734.8 jit_solution(1357443356888814085)
XLA Ops:
  18.4 4.4 all-to-all-start.5
  34.5 9.9 %attend_step.4 = (f32[6,2,512]{2,1,0:T(2,128)}, f32[6,2,512]{2,1,0:T(2,128)}, f32[768,512]{1,0:T(8,128)}) custom-call(s32[1]{0:T(128)} %bitcast.10.refs_0_, s32[1,512]{1,0:T(1,128)} %bitcast.165, bf16[512,768]{1,0:T(8,128)(2,1)} %convolution_convert_fusion.12.refs_2_, bf16[512,768]{1,0:T(8,128)(2,1)} %convolution_convert_fusion.5.refs_3_, ...), custom_call_target="tpu_custom_call" | custom-call | flops 805306368 | bytes 3145728 | tf_op jit(solution)/shard_map/attend_step/pallas_call | solution.py:130
  49.9 5.1 attend_step.5
  55.0 11.4 %collective-permute-done.1 = bf16[512,768]{1,0:T(8,128)(2,1)S(1)} collective-permute-done((bf16[512,768]{1,0:T(8,128)(2,1)S(1)}, bf16[512,768]{1,0:T(8,128)(2,1)S(1)}, u32[]{:S(2)}, u32[]{:S(2)}) %collective-permute-start.1) | collective-permute-done | bytes 786464 | tf_op jit(solution)/shard_map/ppermute | solution.py:394
  70.4 5.2 attend_step.6
  75.6 12.1 %collective-permute-done.2 = bf16[512,768]{1,0:T(8,128)(2,1)S(1)} collective-permute-done((bf16[512,768]{1,0:T(8,128)(2,1)S(1)}, bf16[512,768]{1,0:T(8,128)(2,1)S(1)}, u32[]{:S(2)}, u32[]{:S(2)}) %collective-permute-start.2) | collective-permute-done | bytes 786464 | tf_op jit(solution)/shard_map/ppermute | solution.py:394
  91.4 5.5 attend_step.7
  100.6 4.2 all-to-all-start.1
  109.7 12.0 %all-to-all-done.1.g_ref = bf16[8,2,48,768]{3,2,1,0:T(8,128)(2,1)} async-done(((bf16[8,2,48,768]{3,2,1,0:T(8,128)(2,1)}), bf16[8,2,48,768]{3,2,1,0:T(8,128)(2,1)}, u32[]{:S(2)}, u32[]{:S(2)}) %all-to-all-start.1) | async-done | bytes 1179680 | tf_op jit(solution)/shard_map/all_to_all | solution.py:405
  125.6 4.2 fusion.18
  130.4 3.9 all-to-all-start.2
  139.0 4.3 all-to-all-start
  150.5 9.6 %all-to-all-done.x_ref = bf16[8,2,48,768]{3,2,1,0:T(8,128)(2,1)} async-done(((bf16[8,2,48,768]{3,2,1,0:T(8,128)(2,1)}), bf16[8,2,48,768]{3,2,1,0:T(8,128)(2,1)}, u32[]{:S(2)}, u32[]{:S(2)}) %all-to-all-start) | async-done | bytes 1179680 | tf_op jit(solution)/shard_map/all_to_all | solution.py:405
  160.1 4.7 all-to-all-start.4
  164.8 21.3 %expert_rows.2 = (bf16[8,2,48,768]{3,2,1,0:T(8,128)(2,1)}, bf16[8,2,48,768]{3,2,1,0:T(8,128)(2,1)}, f32[2,384,1]{2,1,0:T(8,128)}) custom-call(bf16[8,2,48,768]{3,2,1,0:T(8,128)(2,1)} %all-to-all-done.x_ref, bf16[8,2,48,768]{3,2,1,0:T(8,128)(2,1)} %all-to-all-done.1.g_ref, f32[2,384,1]{2,1,0:T(8,128)} %reshape.311.gate_ref, bf16[2,768,3072]{2,1,0:T(8,128)(2,1)} %up_ref.2, ...), custom_call_target="tpu_custom_call" | custom-call | flops 14495514624 | bytes 18874368 | tf_op jit(solution)/shard_map/expert_rows/pallas_call | solution.py:279
  190.5 4.2 all-to-all-start.8
  194.7 21.3 %expert_rows.3 = (bf16[8,2,48,768]{3,2,1,0:T(8,128)(2,1)}, bf16[8,2,48,768]{3,2,1,0:T(8,128)(2,1)}, f32[2,384,1]{2,1,0:T(8,128)}) custom-call(bf16[8,2,48,768]{3,2,1,0:T(8,128)(2,1)} %all-to-all-done.4.x_ref.refs_3_, bf16[8,2,48,768]{3,2,1,0:T(8,128)(2,1)} %all-to-all-done.5.g_ref.refs_7_, f32[2,384,1]{2,1,0:T(8,128)} %copy.108.gate_ref, ...), custom_call_target="tpu_custom_call" | custom-call | flops 14495514624 | bytes 18874368 | tf_op jit(solution)/shard_map/expert_rows/pallas_call | solution.py:279
  220.5 9.0 %all_to_all.80 = f32[8,2,48]{2,1,0:T(2,128)} all-to-all(f32[8,2,48]{2,1,0:T(2,128)} %copy.110), channel_id=1, replica_groups=mesh['seq'=4,'exp'=8] {'exp'}, dimensions={0} | all-to-all | bytes 6144 | tf_op jit(solution)/shard_map/all_to_all | solution.py:405
  229.5 21.0 %all_to_all.81 = bf16[8,2,48,768]{3,2,1,0:T(8,128)(2,1)} all-to-all(bf16[8,2,48,768]{3,2,1,0:T(8,128)(2,1)} %get-tuple-element.40), channel_id=1, replica_groups=mesh['seq'=4,'exp'=8] {'exp'}, dimensions={0} | all-to-all | bytes 2359296 | tf_op jit(solution)/shard_map/all_to_all | solution.py:405
  250.5 4.3 all-to-all-start.10
  254.8 5.7 copy.111
  266.0 5.6 all-to-all-done.10
  271.6 4.3 all-to-all-start.11
  279.4 6.3 collective-permute-done.9.refs_8_
  292.8 4.4 all-to-all-start.7
  303.5 10.5 %all-to-all-done.7 = bf16[8,2,48,768]{3,2,1,0:T(8,128)(2,1)} async-done(((bf16[8,2,48,768]{3,2,1,0:T(8,128)(2,1)}), bf16[8,2,48,768]{3,2,1,0:T(8,128)(2,1)}, u32[]{:S(2)}, u32[]{:S(2)}) %all-to-all-start.7) | async-done | bytes 1179680 | tf_op jit(solution)/shard_map/all_to_all | solution.py:405
  314.0 6.6 fusion.39
  327.6 5.3 all-to-all-start.13
  334.7 7.2 all-to-all-done.13
  341.9 4.2 all-to-all-start.12
  350.4 6.2 convolution_convert_fusion.refs_1_.refs_2_.refs_3_
  359.6 57.7 %all-to-all-done.12 = bf16[4,512,192]{1,2,0:T(8,128)(2,1)} async-done(((bf16[4,512,192]{1,2,0:T(8,128)(2,1)}), bf16[4,512,192]{1,2,0:T(8,128)(2,1)}, u32[]{:S(2)}, u32[]{:S(2)}) %all-to-all-start.12) | async-done | bytes 786464 | tf_op jit(solution)/shard_map/all_to_all | solution.py:405
  419.9 32.7 %attend_back.1 = bf16[4,3,192,512]{3,2,1,0:T(8,128)(2,1)} custom-call(s32[4,1,512]{2,1,0:T(1,128)} %bitcast.158, bf16[2048,768]{1,0:T(8,128)(2,1)} %convolution_convert_fusion.refs_1_.refs_2_.refs_3_, bf16[2048,768]{1,0:T(8,128)(2,1)} %convolution_convert_fusion.refs_1_.refs_2_.refs_3_, bf16[2048,768]{1,0:T(8,128)(2,1)} %convolution_convert_fusion.refs_1_.refs_2_.refs_3_, ...), custom_call_target="tpu_custom_call" | custom-call | flops 4026531840 | bytes 6291456 | tf_op jit(solution)/shard_map/attend_back/pallas_call | solution.py:219
  452.5 5.5 bitcast_convert_fusion
  460.3 4.2 all-to-all-start.15
  466.8 33.6 %collective-permute-done.3 = f32[8,2,48]{2,1,0:T(2,128)S(1)} collective-permute-done((f32[8,2,48]{2,1,0:T(2,128)}, f32[8,2,48]{2,1,0:T(2,128)S(1)}, u32[]{:S(2)}, u32[]{:S(2)}) %collective-permute-start.3) | collective-permute-done | bytes 3104 | tf_op jit(solution)/shard_map/ppermute | solution.py:394
  500.3 5.4 collective-permute-done.4
  505.8 4.1 copy.114
  513.3 39.8 %psum.30 = bf16[768,32]{0,1:T(8,128)(2,1)S(1)} all-reduce(bf16[768,32]{0,1:T(8,128)(2,1)S(1)} %convolution_convert_fusion.13), channel_id=1, replica_groups=mesh['seq'=4,'exp'=8] {'seq','exp'}, use_global_device_ids=true, to_apply=%region_21.22 | all-reduce | flops 24576 | bytes 98304 | tf_op jit(solution)/shard_map/psum | solution.py:587
  558.4 40.7 %all-reduce.2 = (f32[768]{0:T(1024)}, f32[4]{0:T(128)S(1)}) all-reduce(f32[768]{0:T(1024)S(1)} %copy-done.39, f32[4]{0:T(128)S(1)} %pad_maximum_fusion.3), channel_id=1, replica_groups=mesh['seq'=4,'exp'=8] {'seq','exp'}, use_global_device_ids=true, to_apply=%region_20.21 | all-reduce | flops 772 | bytes 6176 | tf_op jit(solution)/shard_map/psum | solution.py:590
  607.5 4.8 all-to-all-start.14
  612.3 71.8 %expert_grads.1 = (f32[2,768,3072]{2,1,0:T(8,128)}, f32[2,3072,768]{2,1,0:T(8,128)}) custom-call(f32[2,1536,1]{2,1,0:T(8,128)} %copy.122.refs_0_, bf16[2,768,3072]{2,1,0:T(8,128)(2,1)} %refs_1_.1, bf16[2,3072,768]{2,1,0:T(8,128)(2,1)} %refs_2_.1, bf16[8,2,48,768]{3,2,1,0:T(8,128)(2,1)} %all-to-all-done.4.x_ref.refs_3_, ...), custom_call_target="tpu_custom_call" | custom-call | flops 57982058496 | bytes 56623104 | tf_op jit(solution)/shard_map/expert_grads/pallas_call | solution.py:346
  684.1 5.0 fusion.34
  690.4 7.0 all-gather.3.cloned.1.call-done
  697.5 6.0 copy.116
  703.5 8.2 %reshape.301 = f32[4,768,3,192]{1,0,3,2:T(4,128)} reshape(bf16[3072,576]{0,1:T(8,128)(2,1)} %copy.116) | data formatting | bytes 10616832 | tf_op jit(solution)/shard_map/convert_element_type | solution.py:569
  711.6 4.4 copy.117
  719.5 8.1 %copy.123 = f32[768,2304]{1,0:T(8,128)} copy(f32[768,2304]{0,1:T(8,128)} %bitcast.132) | data formatting | bytes 14155776
  (222 shorter events, 136.2 us)
Async XLA Ops:
  7.2 89.7 %copy-start = (bf16[768,768]{1,0:T(8,128)(2,1)S(1)}, bf16[768,768]{1,0:T(8,128)(2,1)}, u32[]{:S(2)}) copy-start(bf16[768,768]{1,0:T(8,128)(2,1)} %param.19) | copy-start | bytes 3538948
  7.2 37.3 %collective-permute-start = (bf16[512,768]{1,0:T(8,128)(2,1)}, bf16[512,768]{1,0:T(8,128)(2,1)S(1)}, u32[]{:S(2)}, u32[]{:S(2)}) collective-permute-start(bf16[512,768]{1,0:T(8,128)(2,1)} %bitcast.136), channel_id=1, source_target_pairs={{0,8},{8,16},{16,24},{24,0},{1,9},{9,17},{17,25},{25,1},{2,10},{10... | collective-permute-start | bytes 2359304 | tf_op jit(solution)/shard_map/ppermute | solution.py:394
  11.1 15.9 %copy-start.46 = (s32[3,1]{0,1:T(1,128)}, s32[3,1]{0,1:T(1,128)S(1)}, u32[]{:S(2)}) copy-start(s32[3,1]{0,1:T(1,128)S(1)} %broadcast_in_dim.52) | copy-start | bytes 40
  12.4 4.4 copy-start.33
  12.4 4.4 copy-start.35
  18.4 4.4 copy-start.5
  18.4 5.6 copy-start.24
  18.4 82.2 %all-to-all-start.5 = ((bf16[8,2,48,768]{3,2,1,0:T(8,128)(2,1)}), bf16[8,2,48,768]{3,2,1,0:T(8,128)(2,1)}, u32[]{:S(2)}, u32[]{:S(2)}) async-start(bf16[8,2,48,768]{3,2,1,0:T(8,128)(2,1)} %bitcast.26), calls=%async_computation.5 | async-start | bytes 2359296 | tf_op jit(solution)/shard_map/all_to_all | solution.py:405
  24.0 6.8 copy-start.30
  44.7 21.7 %collective-permute-start.1 = (bf16[512,768]{1,0:T(8,128)(2,1)S(1)}, bf16[512,768]{1,0:T(8,128)(2,1)S(1)}, u32[]{:S(2)}, u32[]{:S(2)}) collective-permute-start(bf16[512,768]{1,0:T(8,128)(2,1)S(1)} %collective-permute-done), channel_id=1, source_target_pairs={{0,8},{8,16},{16,24},{24,0},{1,9},{9,17},{17,25},{25,1},{2,10},{10... | collective-permute-start | bytes 2359304 | tf_op jit(solution)/shard_map/ppermute | solution.py:394
  66.6 21.1 %collective-permute-start.2 = (bf16[512,768]{1,0:T(8,128)(2,1)S(1)}, bf16[512,768]{1,0:T(8,128)(2,1)S(1)}, u32[]{:S(2)}, u32[]{:S(2)}) collective-permute-start(bf16[512,768]{1,0:T(8,128)(2,1)S(1)} %collective-permute-done.1), channel_id=1, source_target_pairs={{0,8},{8,16},{16,24},{24,0},{1,9},{9,17},{17,25},{25,1},{2,10},{10... | collective-permute-start | bytes 2359304 | tf_op jit(solution)/shard_map/ppermute | solution.py:394
  100.0 200.6 %copy-start.4 = (f32[512,768]{1,0:T(8,128)}, f32[512,768]{1,0:T(8,128)S(1)}, u32[]{:S(2)}) copy-start(f32[512,768]{1,0:T(8,128)S(1)} %get-tuple-element.101) | copy-start | bytes 4718596
  100.6 21.1 %all-to-all-start.1 = ((bf16[8,2,48,768]{3,2,1,0:T(8,128)(2,1)}), bf16[8,2,48,768]{3,2,1,0:T(8,128)(2,1)}, u32[]{:S(2)}, u32[]{:S(2)}) async-start(bf16[8,2,48,768]{3,2,1,0:T(8,128)(2,1)} %bitcast.138), calls=%async_computation.1 | async-start | bytes 2359296 | tf_op jit(solution)/shard_map/all_to_all | solution.py:405
  121.7 8.7 %all-to-all-start.6 = ((f32[8,2,48]{2,1,0:T(2,128)}), f32[8,2,48]{2,1,0:T(2,128)}, u32[]{:S(2)}, u32[]{:S(2)}) async-start(f32[8,2,48]{2,1,0:T(2,128)} %bitcast.151), calls=%async_computation.6 | async-start | bytes 16384 | tf_op jit(solution)/shard_map/all_to_all | solution.py:405
  130.4 8.7 %all-to-all-start.2 = ((f32[8,2,48]{2,1,0:T(2,128)}), f32[8,2,48]{2,1,0:T(2,128)}, u32[]{:S(2)}, u32[]{:S(2)}) async-start(f32[8,2,48]{2,1,0:T(2,128)} %bitcast.150), calls=%async_computation.2 | async-start | bytes 16384 | tf_op jit(solution)/shard_map/all_to_all | solution.py:405
  139.0 21.1 %all-to-all-start = ((bf16[8,2,48,768]{3,2,1,0:T(8,128)(2,1)}), bf16[8,2,48,768]{3,2,1,0:T(8,128)(2,1)}, u32[]{:S(2)}, u32[]{:S(2)}) async-start(bf16[8,2,48,768]{3,2,1,0:T(8,128)(2,1)} %bitcast.140), calls=%async_computation | async-start | bytes 2359296 | tf_op jit(solution)/shard_map/all_to_all | solution.py:405
  160.1 30.4 %all-to-all-start.4 = ((bf16[8,2,48,768]{3,2,1,0:T(8,128)(2,1)}), bf16[8,2,48,768]{3,2,1,0:T(8,128)(2,1)}, u32[]{:S(2)}, u32[]{:S(2)}) async-start(bf16[8,2,48,768]{3,2,1,0:T(8,128)(2,1)} %bitcast.139), calls=%async_computation.4 | async-start | bytes 2359296 | tf_op jit(solution)/shard_map/all_to_all | solution.py:405
  190.5 29.9 %all-to-all-start.8 = ((f32[8,2,48]{2,1,0:T(2,128)}), f32[8,2,48]{2,1,0:T(2,128)}, u32[]{:S(2)}, u32[]{:S(2)}) async-start(f32[8,2,48]{2,1,0:T(2,128)} %copy.109), calls=%async_computation.8 | async-start | bytes 16384 | tf_op jit(solution)/shard_map/all_to_all | solution.py:405
  250.5 21.1 %all-to-all-start.10 = ((bf16[8,2,48,768]{3,2,1,0:T(8,128)(2,1)}), bf16[8,2,48,768]{3,2,1,0:T(8,128)(2,1)}, u32[]{:S(2)}, u32[]{:S(2)}) async-start(bf16[8,2,48,768]{3,2,1,0:T(8,128)(2,1)} %get-tuple-element.44), calls=%async_computation.10 | async-start | bytes 2359296 | tf_op jit(solution)/shard_map/all_to_all | solution.py:405
  254.8 31.0 %collective-permute-start.9 = (bf16[8,2,48,768]{3,2,1,0:T(8,128)(2,1)}, bf16[8,2,48,768]{3,2,1,0:T(8,128)(2,1)}, u32[]{:S(2)}, u32[]{:S(2)}) collective-permute-start(bf16[8,2,48,768]{3,2,1,0:T(8,128)(2,1)} %all-to-all-done.5.g_ref.refs_7_), channel_id=1, source_target_pairs={{0,8},{8,16},{16,24},{24,0},{1,9},{9,17},{17,25},{25,1},{2,10},{10... | collective-permute-start | bytes 3538952 | tf_op jit(solution)/shard_map/ppermute | solution.py:394
  271.6 21.2 %all-to-all-start.11 = ((bf16[8,2,48,768]{3,2,1,0:T(8,128)(2,1)}), bf16[8,2,48,768]{3,2,1,0:T(8,128)(2,1)}, u32[]{:S(2)}, u32[]{:S(2)}) async-start(bf16[8,2,48,768]{3,2,1,0:T(8,128)(2,1)} %get-tuple-element.45), calls=%async_computation.11 | async-start | bytes 2359296 | tf_op jit(solution)/shard_map/all_to_all | solution.py:405
  285.7 70.8 %collective-permute-start.10 = (bf16[8,2,48,768]{3,2,1,0:T(8,128)(2,1)}, bf16[8,2,48,768]{3,2,1,0:T(8,128)(2,1)}, u32[]{:S(2)}, u32[]{:S(2)}) collective-permute-start(bf16[8,2,48,768]{3,2,1,0:T(8,128)(2,1)} %collective-permute-done.9.refs_8_), channel_id=1, source_target_pairs={{0,8},{8,16},{16,24},{24,0},{1,9},{9,17},{17,25},{25,1},{2,10},{10... | collective-permute-start | bytes 3538952 | tf_op jit(solution)/shard_map/ppermute | solution.py:394
  287.1 61.3 %collective-permute-start.6 = (bf16[8,2,48,768]{3,2,1,0:T(8,128)(2,1)}, bf16[8,2,48,768]{3,2,1,0:T(8,128)(2,1)}, u32[]{:S(2)}, u32[]{:S(2)}) collective-permute-start(bf16[8,2,48,768]{3,2,1,0:T(8,128)(2,1)} %all-to-all-done.4.x_ref.refs_3_), channel_id=1, source_target_pairs={{0,8},{8,16},{16,24},{24,0},{1,9},{9,17},{17,25},{25,1},{2,10},{10... | collective-permute-start | bytes 3538952 | tf_op jit(solution)/shard_map/ppermute | solution.py:394
  292.8 21.3 %all-to-all-start.7 = ((bf16[8,2,48,768]{3,2,1,0:T(8,128)(2,1)}), bf16[8,2,48,768]{3,2,1,0:T(8,128)(2,1)}, u32[]{:S(2)}, u32[]{:S(2)}) async-start(bf16[8,2,48,768]{3,2,1,0:T(8,128)(2,1)} %get-tuple-element.41), calls=%async_computation.7 | async-start | bytes 2359296 | tf_op jit(solution)/shard_map/all_to_all | solution.py:405
  314.0 6.6 copy-start.16
  327.6 14.2 %all-to-all-start.13 = ((f32[4,2,3,1,512]{4,3,2,1,0:T(1,128)}), f32[4,2,3,1,512]{4,3,2,1,0:T(1,128)}, u32[]{:S(2)}, u32[]{:S(2)}) async-start(f32[4,2,3,1,512]{4,3,2,1,0:T(1,128)} %pad_maximum_fusion), calls=%async_computation.13 | async-start | bytes 98304 | tf_op jit(solution)/shard_map/all_to_all | solution.py:405
  334.7 11.4 %copy-start.10 = (bf16[512,768]{1,0:T(8,128)(2,1)S(1)}, bf16[512,768]{1,0:T(8,128)(2,1)}, u32[]{:S(2)}) copy-start(bf16[512,768]{1,0:T(8,128)(2,1)} %copy-done.9) | copy-start | bytes 2359300
  334.7 11.4 %copy-start.26 = (f32[768]{0:T(1024)S(1)}, f32[768]{0:T(1024)}, u32[]{:S(2)}) copy-start(f32[768]{0:T(1024)} %param.17) | copy-start | bytes 9220
  334.7 11.4 %copy-start.42 = (f32[512]{0:T(512)S(1)}, f32[512]{0:T(512)}, u32[]{:S(2)}) copy-start(f32[512]{0:T(512)} %copy-done.41) | copy-start | bytes 6148
  334.7 12.6 %copy-start.44 = (f32[512]{0:T(512)S(1)}, f32[512]{0:T(512)}, u32[]{:S(2)}) copy-start(f32[512]{0:T(512)} %copy-done.43) | copy-start | bytes 6148
  341.9 75.4 %all-to-all-start.12 = ((bf16[4,512,192]{1,2,0:T(8,128)(2,1)}), bf16[4,512,192]{1,2,0:T(8,128)(2,1)}, u32[]{:S(2)}, u32[]{:S(2)}) async-start(bf16[4,512,192]{1,2,0:T(8,128)(2,1)} %fusion.56), calls=%async_computation.12 | async-start | bytes 1572864 | tf_op jit(solution)/shard_map/all_to_all | solution.py:405
  346.1 4.2 copy-start.17
  348.4 116.2 %collective-permute-start.7 = (bf16[8,2,48,768]{3,2,1,0:T(8,128)(2,1)}, bf16[8,2,48,768]{3,2,1,0:T(8,128)(2,1)}, u32[]{:S(2)}, u32[]{:S(2)}) collective-permute-start(bf16[8,2,48,768]{3,2,1,0:T(8,128)(2,1)} %collective-permute-done.6.refs_4_), channel_id=1, source_target_pairs={{0,8},{8,16},{16,24},{24,0},{1,9},{9,17},{17,25},{25,1},{2,10},{10... | collective-permute-start | bytes 3538952 | tf_op jit(solution)/shard_map/ppermute | solution.py:394
  356.6 255.7 %collective-permute-start.11 = (bf16[8,2,48,768]{3,2,1,0:T(8,128)(2,1)}, bf16[8,2,48,768]{3,2,1,0:T(8,128)(2,1)}, u32[]{:S(2)}, u32[]{:S(2)}) collective-permute-start(bf16[8,2,48,768]{3,2,1,0:T(8,128)(2,1)} %collective-permute-done.10.refs_9_), channel_id=1, source_target_pairs={{0,8},{8,16},{16,24},{24,0},{1,9},{9,17},{17,25},{25,1},{2,10},{10... | collective-permute-start | bytes 3538952 | tf_op jit(solution)/shard_map/ppermute | solution.py:394
  458.1 6.7 copy-start.14
  460.3 93.4 %all-to-all-start.15 = ((bf16[8,96,576]{2,1,0:T(8,128)(2,1)}), bf16[8,96,576]{2,1,0:T(8,128)(2,1)}, u32[]{:S(2)}, u32[]{:S(2)}) async-start(bf16[8,96,576]{2,1,0:T(8,128)(2,1)} %bitcast.58), calls=%async_computation.15 | async-start | bytes 1966080 | tf_op jit(solution)/shard_map/all_to_all | solution.py:405
  464.6 140.1 %all-reduce.5.cloned.1.call-start = ((), (), s32[]{:S(2)}) async-start(), calls=%async_computation.16 | async-start | bytes 2359296 | tf_op jit(solution)/shard_map/psum | solution.py:587
  464.6 147.7 %collective-permute-start.8 = (bf16[8,2,48,768]{3,2,1,0:T(8,128)(2,1)}, bf16[8,2,48,768]{3,2,1,0:T(8,128)(2,1)}, u32[]{:S(2)}, u32[]{:S(2)}) collective-permute-start(bf16[8,2,48,768]{3,2,1,0:T(8,128)(2,1)} %collective-permute-done.7.refs_5_), channel_id=1, source_target_pairs={{0,8},{8,16},{16,24},{24,0},{1,9},{9,17},{17,25},{25,1},{2,10},{10... | collective-permute-start | bytes 3538952 | tf_op jit(solution)/shard_map/ppermute | solution.py:394
  466.6 230.9 %all-gather.3.cloned.1.call-start = ((), (), s32[]{:S(2)}) async-start(), calls=%async_computation.17 | async-start | bytes 4055040 | tf_op jit(solution)/shard_map/all_gather | solution.py:567
  466.6 33.7 %collective-permute-start.3 = (f32[8,2,48]{2,1,0:T(2,128)}, f32[8,2,48]{2,1,0:T(2,128)S(1)}, u32[]{:S(2)}, u32[]{:S(2)}) collective-permute-start(f32[8,2,48]{2,1,0:T(2,128)} %all-to-all-done.6), channel_id=1, source_target_pairs={{0,8},{8,16},{16,24},{24,0},{1,9},{9,17},{17,25},{25,1},{2,10},{10... | collective-permute-start | bytes 9224 | tf_op jit(solution)/shard_map/ppermute | solution.py:394
  500.3 5.4 collective-permute-start.4
  505.8 5.5 collective-permute-start.5
  505.8 5.6 copy-start.29
  513.1 45.3 %copy-start.39 = (f32[768]{0:T(1024)S(1)}, f32[768]{0:T(1024)}, u32[]{:S(2)}) copy-start(f32[768]{0:T(1024)} %get-tuple-element.90) | copy-start | bytes 9220
  607.5 76.6 %all-to-all-start.14 = ((bf16[4,576,512]{2,1,0:T(8,128)(2,1)}), bf16[4,576,512]{2,1,0:T(8,128)(2,1)}, u32[]{:S(2)}, u32[]{:S(2)}) async-start(bf16[4,576,512]{2,1,0:T(8,128)(2,1)} %bitcast.144), calls=%async_computation.14 | async-start | bytes 4718592 | tf_op jit(solution)/shard_map/all_to_all | solution.py:405
  612.3 71.8 %copy-start.32 = (f32[512]{0:T(512)S(1)}, f32[512]{0:T(512)}, u32[]{:S(2)}) copy-start(f32[512]{0:T(512)} %copy-done.30) | copy-start | bytes 6148
  711.6 4.4 copy-start.3
  719.5 8.1 %copy-start.1 = (bf16[768,768]{1,0:T(8,128)(2,1)S(1)}, bf16[768,768]{1,0:T(8,128)(2,1)}, u32[]{:S(2)}) copy-start(bf16[768,768]{1,0:T(8,128)(2,1)} %param.19) | copy-start | bytes 3538948
  (27 other events, 60.0 us)
Sparse Core Ops, SparseCore 0:
  471.4 133.2 all-reduce.4
  608.0 89.4 all-gather.2

commit v2 on v0

v2 whole, which is shorter than its diff:
```python
import jax
import jax.numpy as jnp
from jax import lax
from jax.experimental import pallas as pl
from jax.experimental.pallas import tpu as pltpu
from jax.sharding import PartitionSpec as P

D = 768
HEADS = 12
HEAD = 64
EXPERTS = 32
FROZEN = 16
CAP = 48

EPS = 1e-06
MASKED = -1e30
BF = jnp.bfloat16
F32 = jnp.float32
TANH_A = 0.7978845608028654
TANH_B = 0.044715
GRAD_ROWS = 1536
GRAD_TILE = 768
MISC = 896
VMEM_BYTES = 56 * 1024 * 1024


def mm(a, b):
    return jnp.dot(a, b, preferred_element_type=F32)


def mm_nt(a, b):
    return lax.dot_general(a, b, (((1,), (1,)), ((), ())), preferred_element_type=F32)


def ein(form, a, b):
    return jnp.einsum(form, a, b, preferred_element_type=F32)


def mm_tn(a, b):
    return lax.dot_general(a, b, (((0,), (0,)), ((), ())), preferred_element_type=F32)


def params():
    return pltpu.CompilerParams(vmem_limit_bytes=VMEM_BYTES)


def cost(micros):
    return pl.CostEstimate(flops=int(micros * 1.1e9), bytes_accessed=0, transcendentals=0)


def whole(shape):
    return pl.BlockSpec(shape, lambda *unused: (0,) * len(shape))


def called(
    kernel,
    name,
    outs,
    info,
    operands,
    in_specs=None,
    scratch=(),
    micros=5,
    grid=(1,),
    out_specs=None,
    aliases=None,
    deps=(),
    through=(),
):
    specs = [None] * len(operands) if in_specs is None else in_specs
    specs = [whole(a.shape) if b is None else b for a, b in zip(operands, specs)]
    results = [whole(shape) for shape, unused in outs] if out_specs is None else list(out_specs)
    shapes = [jax.ShapeDtypeStruct(shape, kind) for shape, kind in outs]
    shapes += [jax.ShapeDtypeStruct(a.shape, a.dtype) for a in through]
    held = pl.BlockSpec(memory_space=pl.ANY)
    aliases = dict(aliases or {})
    for i in range(len(through)):
        aliases[1 + len(operands) + i] = len(outs) + i
    extra = len(through) + len(deps)

    def inner(info_ref, *refs):
        ins, rest = refs[: len(operands)], refs[len(operands) + extra :]
        kernel(info_ref, *ins, *rest[: len(outs)], *rest[len(outs) + len(through) :])

    call = pl.pallas_call(
        inner,
        out_shape=shapes,
        grid_spec=pltpu.PrefetchScalarGridSpec(
            num_scalar_prefetch=1,
            grid=grid,
            in_specs=specs + [held] * extra,
            out_specs=results + [held] * len(through),
            scratch_shapes=list(scratch),
        ),
        input_output_aliases=aliases,
        compiler_params=params(),
        cost_estimate=cost(micros),
        name=name,
    )
    return list(call(info, *operands, *through, *deps))


INFO = 2


def doc_start(info_ref, position):
    bound = 0
    start = jnp.zeros_like(position)
    for i in range(INFO, info_ref.shape[0]):
        bound = bound + info_ref[i]
        start = jnp.where(position >= bound, bound, start)
    return start


def doc_end(info_ref):
    bound = 0
    for i in range(INFO, info_ref.shape[0]):
        bound = bound + info_ref[i]
    return bound


def need_mask(info_ref, key_start, last_query):
    return doc_start(info_ref, jnp.full((1, 128), last_query, jnp.int32))[0, 0] > key_start


def route_kernel(local, info_ref, routes_ref, g_ref, pick_ref, train_ref, frozen_ref):
    tok = g_ref.shape[0]
    half = pick_ref.shape[0] // 2
    first, second = routes_ref[0:1, :], routes_ref[1:2, :]
    row = lax.broadcasted_iota(jnp.int32, (EXPERTS, tok), 0)
    expert = jnp.where(row < FROZEN, row + FROZEN, row - FROZEN)
    position = info_ref[0] * tok + lax.broadcasted_iota(jnp.int32, (EXPERTS, tok), 1)
    live = ((expert == first) | (expert == second)) & (position < doc_end(info_ref))
    earlier = lax.broadcasted_iota(jnp.int32, (tok, tok), 0) < lax.broadcasted_iota(
        jnp.int32, (tok, tok), 1
    )
    place = mm(jnp.where(live, 1.0, 0.0).astype(BF), jnp.where(earlier, 1.0, 0.0).astype(BF))
    place = jnp.where(live, place, -1.0)
    slot = lax.broadcasted_iota(jnp.int32, (CAP, tok), 0).astype(F32)
    sums = jnp.broadcast_to((first + second).astype(F32), (16, tok)).astype(BF)
    sum_row = lax.broadcasted_iota(jnp.int32, (16, CAP), 0)
    for part, out_ref in ((0, train_ref), (1, frozen_ref)):
        for d in range(FROZEN // local):
            found = jnp.zeros((16, CAP), F32)
            for i in range(local):
                e = part * FROZEN + d * local + i
                taken = jnp.where(place[e : e + 1, :] == slot, 1.0, 0.0).astype(BF)
                pick_ref[e * CAP : (e + 1) * CAP, :] = taken
                found = jnp.where(sum_row == i, mm_nt(sums, taken), found)
            out_ref[d, local * CAP :, :] = jnp.zeros((16, D), BF)
            out_ref[d, local * CAP :, 0:CAP] = found.astype(BF)
        rows = mm(pick_ref[part * half : (part + 1) * half, :], g_ref[...]).astype(BF)
        for d in range(FROZEN // local):
            out_ref[d, : local * CAP, :] = rows[d * local * CAP : (d + 1) * local * CAP, :]


def route(info, local, routes, g):
    tok = g.shape[0]
    sent = (FROZEN // local, local * CAP + 16, D)

    def kernel(*refs):
        route_kernel(local, *refs)

    return called(
        kernel,
        "route",
        [((EXPERTS * CAP, tok), BF), (sent, BF), (sent, BF)],
        info,
        [routes, g],
        [None, None],
        micros=6,
    )


def slot_sums(tile, local_id):
    parts = []
    for i in range(tile.shape[0]):
        turned = tile[i].astype(F32).T
        lane = lax.broadcasted_iota(jnp.int32, turned.shape, 1)
        column = jnp.sum(jnp.where(lane == local_id, turned, 0.0), axis=1, keepdims=True)
        parts.append(column[:CAP, :])
    return jnp.concatenate(parts, axis=0)


def gelu_parts(h):
    h2 = h * h
    t = jnp.tanh(h * (TANH_A + (TANH_A * TANH_B) * h2))
    half = 0.5 * t + 0.5
    act = h * half
    slope = half + act * (1.0 - half) * (2.0 * TANH_A + (6.0 * TANH_A * TANH_B) * h2)
    return act, slope


def attend_kernel(step, last, info_ref, x_ref, gain_ref, w_q_ref, w_k_ref, w_v_ref, *refs):
    first = step == 0
    refs = list(refs)
    if first:
        n1_ref, q_ref = refs[:2]
        refs = refs[2:]
    else:
        q_ref, m_in, l_in, acc_in, n1_ref = refs[:5]
        refs = refs[5:]
    if last:
        attn_ref = refs.pop(0)
        l_ref = refs.pop(0)
        m_ref, acc_ref, k_all, v_all = refs
    else:
        m_ref, l_ref, acc_ref, k_all, v_all = refs
    block = info_ref[0] - step
    rows = x_ref.shape[0]
    pairs = k_all.shape[0]

    x = x_ref[...].astype(F32)
    n1 = x * lax.rsqrt(jnp.mean(x * x, axis=1, keepdims=True) + EPS) * gain_ref[...]
    n1_ref[...] = n1.astype(BF)

    def project():
        n1 = n1_ref[...]
        for i in range(pairs // 2):
            cols = slice(i * 4 * HEAD, (i + 1) * 4 * HEAD)
            k = mm(n1, w_k_ref[:, cols]).astype(BF)
            v = mm(n1, w_v_ref[:, cols]).T.astype(BF)
            for j in range(2):
                k_all[2 * i + j] = k[:, j * 2 * HEAD : (j + 1) * 2 * HEAD]
                v_all[2 * i + j] = v[j * 2 * HEAD : (j + 1) * 2 * HEAD, :]
            if first:
                q = mm(n1, w_q_ref[:, cols]).astype(BF) * jnp.asarray(HEAD**-0.5, BF)
                for j in range(2):
                    q_ref[2 * i + j] = q[:, j * 2 * HEAD : (j + 1) * 2 * HEAD]

    def attend(masked):
        key_pos = block * rows + lax.broadcasted_iota(jnp.int32, (rows, rows), 0)
        query_pos = info_ref[0] * rows + lax.broadcasted_iota(jnp.int32, (1, rows), 1)
        start = doc_start(info_ref, query_pos)

        def pair(p, carry):
            q = q_ref[p]
            k = k_all[p]
            lane = lax.broadcasted_iota(jnp.int32, q.shape, 1)
            zero = jnp.zeros_like(q)
            found = [
                mm_nt(k, jnp.where(lane < HEAD, q, zero)),
                mm_nt(k, jnp.where(lane < HEAD, zero, q)),
            ]
            for half in range(2):
                scores = found[half]
                if masked:
                    allowed = key_pos >= start
                    if first:
                        allowed = allowed & (key_pos <= query_pos)
                    scores = jnp.where(allowed, scores, MASKED)
                top = jnp.max(scores, axis=0, keepdims=True)
                if not first:
                    old = m_in[p, half : half + 1, :]
                    top = jnp.maximum(top, old)
                probs = jnp.exp(scores - top)
                total = jnp.sum(probs, axis=0, keepdims=True)
                value = mm(v_all[p, half * HEAD : (half + 1) * HEAD, :], probs.astype(BF))
                part = pl.ds(pl.multiple_of(p * 2 * HEAD + half * HEAD, HEAD), HEAD)
                if not first:
                    decay = jnp.exp(old - top)
                    total = total + l_in[p, half : half + 1, :] * decay
                    value = value + acc_in[part, :] * decay
                m_ref[p, half : half + 1, :] = top
                l_ref[p, half : half + 1, :] = total
                acc_ref[part, :] = value
            return carry

        lax.fori_loop(0, pairs, pair, 0)

    if first:
        project()
        attend(True)
    else:
        masked = need_mask(info_ref, block * rows, info_ref[0] * rows + rows - 1)

        @pl.when(block >= 0)
        def _():
            project()

        @pl.when((block >= 0) & masked)
        def _():
            attend(True)

        @pl.when((block >= 0) & jnp.logical_not(masked))
        def _():
            attend(False)

        @pl.when(block < 0)
        def _():
            m_ref[...] = m_in[...]
            l_ref[...] = l_in[...]
            acc_ref[...] = acc_in[...]

    if last:
        for p in range(pairs):
            for half in range(2):
                part = slice((2 * p + half) * HEAD, (2 * p + half + 1) * HEAD)
                total = l_ref[p, half : half + 1, :]
                acc_ref[part, :] = acc_ref[part, :] / total
                l_ref[p, half : half + 1, :] = m_ref[p, half : half + 1, :] + jnp.log(total)
            part = slice(p * 2 * HEAD, (p + 1) * 2 * HEAD)
            attn_ref[:, part] = acc_ref[part, :].T.astype(BF)


def attend_step(step, last, info, x, gain, w, state, deps=(), through=()):
    tok = x.shape[0]
    pairs = HEADS // 2
    stat, acc = ((pairs, 2, tok), F32), ((D, tok), F32)
    row, by_pair = ((tok, D), BF), ((pairs, tok, 2 * HEAD), BF)
    outs = [row] + ([by_pair] if step == 0 else []) + ([row, stat] if last else [stat, stat, acc])
    scratch = [pltpu.VMEM(*by_pair), pltpu.VMEM((pairs, 2 * HEAD, tok), BF)]
    if last:
        scratch = [pltpu.VMEM(*stat), pltpu.VMEM(*acc)] + scratch

    def kernel(*refs):
        attend_kernel(step, last, *refs)

    square = (D, D)
    return called(
        kernel,
        "attend_step",
        outs,
        info,
        [x, gain, w, w, w, *state],
        [
            None,
            None,
            pl.BlockSpec(square, lambda i, r: (0, 0)),
            pl.BlockSpec(square, lambda i, r: (0, 1)),
            pl.BlockSpec(square, lambda i, r: (0, 2)),
        ]
        + [None] * len(state),
        scratch,
        micros=13,
        deps=deps,
        through=through,
    )


def attend_back_kernel(blocks, heads, info_ref, qkv_ref, misc_ref, *refs):
    n1_refs, do_refs, out_refs = [refs[i * blocks : (i + 1) * blocks] for i in range(3)]
    part_ref, dq_ref, dk_ref, dv_ref, k_mine, v_mine, k_t, do_all, lse_all, delta_all, out_all = refs[
        3 * blocks :
    ]
    rows = qkv_ref.shape[0] // blocks
    tiles, deep, width = do_refs[0].shape
    lane = lax.broadcasted_iota(jnp.int32, (rows, 2 * HEAD), 1)
    dq_ref[...] = jnp.zeros_like(dq_ref)

    def turn(b):
        return lax.rem(info_ref[0] - b + blocks, blocks)

    for b in range(blocks):
        do_all[b] = do_refs[b][:, :width, :].reshape(rows, width)
        stats = [do_refs[b][t, width:, :].astype(F32) for t in range(tiles)]
        stats = jnp.concatenate(stats, axis=1)
        delta_all[b] = stats[:heads] + stats[heads : 2 * heads]
        lse_all[b] = stats[2 * heads : 3 * heads] + stats[3 * heads : 4 * heads]

    def key_step(kb, carry):
        kt = turn(kb)
        key_rows = pl.ds(pl.multiple_of(kt * rows, rows), rows)
        for h in range(heads):
            first = (h // 2) * 2 * HEAD
            k = qkv_ref[key_rows, width + first : width + first + 2 * HEAD]
            v = qkv_ref[key_rows, 2 * width + first : 2 * width + first + 2 * HEAD]
            mine = (lane < HEAD) if h % 2 == 0 else (lane >= HEAD)
            zero = jnp.zeros_like(k)
            k_mine[h] = jnp.where(mine, k, zero)
            v_mine[h] = jnp.where(mine, v, zero)
            k_t[h] = k.T[(h % 2) * HEAD : (h % 2 + 1) * HEAD, :]
        dk_ref[...] = jnp.zeros_like(dk_ref)
        dv_ref[...] = jnp.zeros_like(dv_ref)

        def pair(qb, diagonal, masked):
            qt = turn(qb)
            query_rows = pl.ds(pl.multiple_of(qt * rows, rows), rows)
            if masked:
                key_pos = kb * rows + lax.broadcasted_iota(jnp.int32, (rows, rows), 0)
                query_pos = qb * rows + lax.broadcasted_iota(jnp.int32, (1, rows), 1)
                allowed = key_pos >= doc_start(info_ref, query_pos)
                if diagonal:
                    allowed = allowed & (key_pos <= query_pos)

            def of_head(h):
                cols = slice((h // 2) * 2 * HEAD, (h // 2 + 1) * 2 * HEAD)
                return qkv_ref[query_rows, cols], do_all[qt, :, cols]

            def products(h):
                q, do = of_head(h)
                return mm_nt(k_mine[h], q), mm_nt(v_mine[h], do)

            later = products(0)
            for h in range(heads):
                scores, dprobs = later
                if h + 1 < heads:
                    later = products(h + 1)
                q, do = of_head(h)
                probs = jnp.exp(scores - lse_all[qt, h : h + 1, :])
                if masked:
                    probs = jnp.where(allowed, probs, 0.0)
                dscores = (probs * (dprobs - delta_all[qt, h : h + 1, :])).astype(BF)
                dv_ref[h] += mm(probs.astype(BF), do)
                dk_ref[h] += mm(dscores, q)
                dq_ref[qt, h] += mm(k_t[h], dscores)

        pair(kb, True, True)

        def query_step(qb, carry):
            masked = need_mask(info_ref, kb * rows, qb * rows + rows - 1)

            @pl.when(masked)
            def _():
                pair(qb, False, True)

            @pl.when(jnp.logical_not(masked))
            def _():
                pair(qb, False, False)

            return carry

        lax.fori_loop(kb + 1, blocks, query_step, 0)
        for h in range(heads):
            part = slice((h % 2) * HEAD, (h % 2 + 1) * HEAD)
            for i, grad_ref in ((1, dk_ref), (2, dv_ref)):
                at = (i * heads + h) * HEAD
                out_all[kt, at : at + HEAD, :] = grad_ref[h].T[part, :].astype(BF)
        return carry

    lax.fori_loop(0, blocks, key_step, 0)
    total = 0.0
    for b in range(blocks):
        for h in range(heads):
            out_all[b, h * HEAD : (h + 1) * HEAD, :] = (dq_ref[b, h] * HEAD**-0.5).astype(BF)
        grads = out_all[b]
        out_refs[b][...] = grads
        total = total + mm(grads, n1_refs[b][...])
    part_ref[:, :MISC] = misc_ref[...]
    part_ref[:, MISC:] = total.T.astype(BF)


def attend_back(heads, info, qkv, misc, n1, dos, deps):
    rows = qkv.shape[0]
    blocks = len(dos)
    tiles, deep, width = dos[0].shape
    tok = rows // blocks
    cols = 3 * heads * HEAD

    def kernel(*refs):
        attend_back_kernel(blocks, heads, *refs)

    *grads, part = called(
        kernel,
        "attend_back",
        [((cols, tok), BF)] * blocks + [((D, MISC + cols), BF)],
        info,
        [qkv, misc, *n1, *dos],
        scratch=[
            pltpu.VMEM((blocks, heads, HEAD, tok), F32),
            pltpu.VMEM((heads, tok, 2 * HEAD), F32),
            pltpu.VMEM((heads, tok, 2 * HEAD), F32),
            pltpu.VMEM((heads, tok, 2 * HEAD), BF),
            pltpu.VMEM((heads, tok, 2 * HEAD), BF),
            pltpu.VMEM((heads, HEAD, tok), BF),
            pltpu.VMEM((blocks, tok, width), BF),
            pltpu.VMEM((blocks, heads, tok), F32),
            pltpu.VMEM((blocks, heads, tok), F32),
            pltpu.VMEM((blocks, cols, tok), BF),
        ],
        micros=32,
        deps=deps,
    )
    return grads, part


def project_back_kernel(blocks, info_ref, w_ref, *refs):
    out_ref = refs[blocks]
    rows = refs[0].shape[0]
    for b in range(blocks):
        out_ref[b * rows : (b + 1) * rows, :] = mm_nt(refs[b][...], w_ref[...]).astype(BF)


def project_back(info, w, n1, deps, through):
    blocks = len(n1)

    def kernel(*refs):
        project_back_kernel(blocks, *refs)

    shape = (blocks * n1[0].shape[0], w.shape[0])
    return called(
        kernel, "project_back", [(shape, BF)], info, [w, *n1], micros=1, deps=deps, through=through
    )


def slot_gate(own, sums, x, router):
    lane = lax.broadcasted_iota(jnp.int32, (x.shape[0], router.shape[1]), 1)
    other = sums.astype(jnp.int32) - own
    signs = jnp.where(lane == own, 1.0, 0.0) - jnp.where(lane == other, 1.0, 0.0)
    margin = jnp.sum(mm(x, router) * signs, axis=1, keepdims=True)
    return 1.0 / (1.0 + jnp.exp(-margin)), signs


def expert_kernel(
    first_id,
    info_ref,
    x_ref,
    g_ref,
    sums_ref,
    router_ref,
    up_ref,
    down_ref,
    mix_ref,
    dx_ref,
    do_ref,
    drouter_ref,
    xs,
    dos,
    gate_ref,
    signs_ref,
    eacc,
    dacc,
):
    expert = pl.program_id(0)
    step = pl.program_id(1)
    rows = xs.shape[0]
    block = x_ref.shape

    @pl.when(step == 0)
    def _():
        x = x_ref[...].reshape(rows, D)
        xs[...] = x
        own = first_id + info_ref[1] * pl.num_programs(0) + expert
        gate, signs = slot_gate(own, slot_sums(sums_ref, expert), x, router_ref[...])
        gate_ref[...] = gate
        signs_ref[...] = signs
        do = (gate * g_ref[...].reshape(rows, D).astype(F32)).astype(BF)
        dos[...] = do
        do_ref[...] = do.reshape(block)

    act, slope = gelu_parts(mm(xs[...], up_ref[0]))
    dhid = (mm_nt(dos[...], down_ref[0]) * slope).astype(BF)
    out = mm(act.astype(BF), down_ref[0])
    dx = mm_nt(dhid, up_ref[0])

    @pl.when(step == 0)
    def _():
        eacc[...] = out
        dacc[...] = dx

    @pl.when(step > 0)
    def _():
        eacc[...] += out
        dacc[...] += dx

    @pl.when(step == pl.num_programs(1) - 1)
    def _():
        out = eacc[...]
        gate = gate_ref[...]
        g = g_ref[...].reshape(rows, D).astype(F32)
        mix_ref[...] = (gate * out).astype(BF).reshape(block)
        dgate = jnp.sum(g * out, axis=1, keepdims=True)
        dlogits = (gate * (1.0 - gate) * dgate * signs_ref[...]).astype(BF)
        dx_ref[...] = (dacc[...] + mm_nt(dlogits, router_ref[...])).astype(BF).reshape(block)
        drouter = mm_tn(dlogits, xs[...])

        @pl.when(expert == 0)
        def _():
            drouter_ref[...] = drouter

        @pl.when(expert > 0)
        def _():
            drouter_ref[...] += drouter


def expert_rows(first_id, info, x, g, router, up, down, deps, through=()):
    sources, experts = x.shape[:2]
    rows = sources * CAP
    hidden = up.shape[2]
    tile = 1536
    row_spec = pl.BlockSpec((sources, 1, CAP, D), lambda e, f, r: (0, e, 0, 0))

    def kernel(*refs):
        expert_kernel(first_id, *refs)

    return called(
        kernel,
        "expert_rows",
        [(x.shape, BF), (x.shape, BF), (x.shape, BF), ((router.shape[1], D), F32)],
        info,
        [x, g, g, router, up, down],
        [
            row_spec,
            pl.BlockSpec((sources, CAP, D), lambda e, f, r: (0, e, 0)),
            pl.BlockSpec((sources, 16, 128), lambda e, f, r: (0, experts * CAP // 16, 0)),
            None,
            pl.BlockSpec((1, D, tile), lambda e, f, r: (e, 0, f)),
            pl.BlockSpec((1, tile, D), lambda e, f, r: (e, f, 0)),
        ],
        [
            pltpu.VMEM((rows, D), BF),
            pltpu.VMEM((rows, D), BF),
            pltpu.VMEM((rows, 1), F32),
            pltpu.VMEM((rows, 128), F32),
            pltpu.VMEM((rows, D), F32),
            pltpu.VMEM((rows, D), F32),
        ],
        micros=23,
        grid=(experts, hidden // tile),
        out_specs=[row_spec, row_spec, row_spec, whole((router.shape[1], D))],
        deps=deps,
        through=through,
    )


def gated_kernel(count, info_ref, router_ref, *refs):
    x_refs, g_refs, sum_refs, out_refs = [refs[i * count : (i + 1) * count] for i in range(4)]
    sources, experts = x_refs[0].shape[:2]
    for b in range(count):
        for e in range(experts):
            own = FROZEN + info_ref[1] * experts + e
            x = x_refs[b][:, e].reshape(sources * CAP, D)
            gate, unused = slot_gate(own, slot_sums(sum_refs[b], e), x, router_ref[...])
            g = g_refs[b][:, e * CAP : (e + 1) * CAP, :].reshape(sources * CAP, D).astype(F32)
            out_refs[b][:, e] = (gate * g).astype(BF).reshape(sources, CAP, D)


def gated(info, router, xs, gs, sums, deps=()):
    count = len(xs)

    def kernel(*refs):
        gated_kernel(count, *refs)

    return called(
        kernel,
        "gated",
        [(x.shape, BF) for x in xs],
        info,
        [router, *xs, *gs, *sums],
        micros=1,
        deps=deps,
    )


def expert_grad_kernel(group, add, info_ref, ins, dup_ref, ddown_ref, done_ref, xs, dos):
    up_ref, down_ref = ins[:2]
    x_refs, do_refs = ins[2 : 2 + group], ins[2 + group : 2 + 2 * group]
    rows = xs.shape[0] // group

    @pl.when(pl.program_id(0) == 0)
    def _():
        done_ref[...] = jnp.zeros_like(done_ref)
        for b in range(group):
            part = slice(b * rows, (b + 1) * rows)
            xs[part, :] = x_refs[b][...].reshape(rows, D)
            dos[part, :] = do_refs[b][...].reshape(rows, D)

    act, slope = gelu_parts(mm(xs[...], up_ref[0]))
    dhid = (mm_nt(dos[...], down_ref[0]) * slope).astype(BF)
    ddown = mm_tn(act.astype(BF), dos[...])
    dup = mm_tn(xs[...], dhid)
    if add:
        ddown = ddown + ins[-1][0]
        dup = dup + ins[-2][0]
    ddown_ref[0] = ddown
    dup_ref[0] = dup


def expert_grads(expert, span, first, group, info, xs, dos, up, down, totals, deps, through):
    sources, experts = xs[0].shape[:2]
    rows = group * sources * CAP
    tile = GRAD_TILE
    start, count = span
    add = first > 0
    up_spec = pl.BlockSpec((1, D, tile), lambda f, r: (expert, 0, start + f))
    down_spec = pl.BlockSpec((1, tile, D), lambda f, r: (expert, start + f, 0))
    in_specs = [up_spec, down_spec]
    in_specs += [pl.BlockSpec((sources, 1, CAP, D), lambda f, r: (0, expert, 0, 0))] * (2 * group)
    part = slice(first, first + group)
    operands = [up, down, *xs[part], *dos[part]]
    aliases = {}
    if totals is not None:
        aliases = {1 + len(operands): 0, 2 + len(operands): 1}
        in_specs += [up_spec, down_spec] if add else [pl.BlockSpec(memory_space=pl.ANY)] * 2
        operands += list(totals)

    def kernel(info_ref, *refs):
        ins, rest = refs[: len(operands)], refs[len(operands) :]
        expert_grad_kernel(group, add, info_ref, ins, *rest)

    return called(
        kernel,
        "expert_grads",
        [(up.shape, F32), (down.shape, F32), ((8, 128), F32)],
        info,
        operands,
        in_specs,
        [pltpu.VMEM((rows, D), BF), pltpu.VMEM((rows, D), BF)],
        micros=9 * count,
        grid=(count,),
        out_specs=[up_spec, down_spec, whole((8, 128))],
        aliases=aliases,
        deps=deps,
        through=through,
    )


def expert_grads_part(expert, span, info, xs, dos, up, down, totals, deps, through):
    blocks = len(xs)
    sources, experts = xs[0].shape[:2]
    group = max(1, min(blocks, GRAD_ROWS // (sources * CAP)))
    for first in range(0, blocks, group):
        dup, ddown, done, *through = expert_grads(
            expert, span, first, group, info, xs, dos, up, down, totals, deps, through
        )
        totals = [dup, ddown]
    return totals, [done, *through]


def token_forward_kernel(
    info_ref, attn_ref, x_ref, gain_ref, w_ref, pick_ref, mid_ref, square_ref, train_ref, frozen_ref
):
    tok = x_ref.shape[0]
    half = pick_ref.shape[0] // 2
    branch = mm(attn_ref[...], w_ref[...])
    mid = x_ref[...].astype(F32) + branch
    mid_ref[...] = mid
    r = lax.rsqrt(jnp.mean(mid * mid, axis=1, keepdims=True) + EPS)
    n2 = (mid * r * gain_ref[...]).astype(BF)
    train_ref[...] = mm(pick_ref[:half, :], n2).astype(BF)
    frozen_ref[...] = mm(pick_ref[half:, :], n2).astype(BF)
    position = info_ref[0] * tok + lax.broadcasted_iota(jnp.int32, (tok, D), 0)
    square = jnp.where(position < doc_end(info_ref), branch * branch, 0.0)
    square_ref[...] = jnp.sum(square, axis=0, keepdims=True)


def token_forward(info, attn, x, gain, w, pick):
    tok = x.shape[0]
    half = ((pick.shape[0] // 2, D), BF)
    return called(
        token_forward_kernel,
        "token_forward",
        [((tok, D), F32), ((1, D), F32), half, half],
        info,
        [attn, x, gain, w, pick],
        [None] * 5,
        micros=6,
    )


def token_back_kernel(
    heads,
    groups,
    info_ref,
    pick_ref,
    dx_t_ref,
    dx_f_ref,
    mid_ref,
    g_ref,
    gain_ref,
    w_ref,
    wg_ref,
    attn_ref,
    lse_ref,
    head_ref,
    *refs,
):
    send_refs = refs[:groups]
    dmid_ref, dbranch_ref, dgain_ref = refs[groups:]
    tiles, deep, width = send_refs[0].shape
    tok = mid_ref.shape[0]
    half = pick_ref.shape[0] // 2

    dn2 = mm_tn(pick_ref[:half, :], dx_t_ref[...].reshape(half, D))
    dn2 = dn2 + mm_tn(pick_ref[half:, :], dx_f_ref[...].reshape(half, D))
    mid = mid_ref[...]
    r = lax.rsqrt(jnp.mean(mid * mid, axis=1, keepdims=True) + EPS)
    u = mid * r
    dgain_ref[...] = jnp.sum(dn2 * u, axis=0, keepdims=True)
    scaled = dn2 * gain_ref[...]
    dmid = g_ref[...].astype(F32) + r * (scaled - u * jnp.mean(scaled * u, axis=1, keepdims=True))
    dmid_ref[...] = dmid
    dbranch = dmid.astype(BF)
    dbranch_ref[...] = dbranch

    dattn = mm_nt(dbranch, w_ref[...]).astype(BF).astype(F32)
    prod = dattn * attn_ref[...].astype(F32)
    high = prod.astype(BF)
    low = (prod - high.astype(F32)).astype(BF)
    for turn in range(groups):
        g = lax.rem(info_ref[0] + turn, groups)
        sent = mm_nt(dbranch, wg_ref[g]).astype(BF)
        delta = mm_nt(head_ref[g], high) + mm_nt(head_ref[g], low)
        parts = []
        for stat in (delta[:heads], lse_ref[g][:heads]):
            high_part = stat.astype(BF).astype(F32)
            parts += [high_part, stat - high_part]
        blank = jnp.zeros((16 - 4 * heads, tok), F32)
        stats = jnp.concatenate(parts + [blank], axis=0).astype(BF)
        for t in range(tiles):
            part = slice(t * width, (t + 1) * width)
            send_refs[turn][t, :width, :] = sent[part, :]
            send_refs[turn][t, width:, :] = stats[:, part]


def token_back(
    heads, groups, width, info, pick, dx_t, dx_f, mid, g, gain, w, w_groups, attn, lse, head_rows, deps
):
    tok = mid.shape[0]
    tiles = tok // width

    def kernel(*refs):
        token_back_kernel(heads, groups, *refs)

    outs = [((tiles, width + 16, width), BF)] * groups
    operands = [pick, dx_t, dx_f, mid, g, gain, w, w_groups, attn, lse, head_rows]
    found = called(
        kernel,
        "token_back",
        outs + [((tok, D), F32), ((tok, D), BF), ((1, D), F32)],
        info,
        operands,
        micros=10,
        deps=deps,
    )
    return [found[:groups]] + found[groups:]


def token_mix_kernel(
    info_ref, pick_ref, mix_ref, mid_ref, x_ref, attn_ref, dbranch_ref, rt_ref, rf_ref, dgain_ref, square_ref, out_ref, misc_ref
):
    tok = mid_ref.shape[0]
    half = pick_ref.shape[0] // 2
    mix = 0.0
    for i in range(2):
        rows = mix_ref[:, i].reshape(half, D)
        mix = mix + mm_tn(pick_ref[i * half : (i + 1) * half, :], rows)
    out_ref[...] = (mid_ref[...] + mix).astype(BF)
    valid = info_ref[0] * tok + lax.broadcasted_iota(jnp.int32, (tok, D), 0) < doc_end(info_ref)
    x = x_ref[...].astype(F32)
    stats = [
        jnp.sum(jnp.where(valid, x * x, 0.0)),
        jnp.sum(square_ref[...]),
        jnp.sum(jnp.where(valid, mix * mix, 0.0)),
        jnp.clip(doc_end(info_ref) - info_ref[0] * tok, 0, tok).astype(F32),
    ]
    misc_ref[:, :D] = mm_tn(attn_ref[...], dbranch_ref[...]).astype(BF)
    tail = (rt_ref[...] + rf_ref[...]).T
    gains = jnp.broadcast_to(dgain_ref[...], (8, D)).T[:, 0:1]
    row = lax.broadcasted_iota(jnp.int32, tail.shape, 0)
    lane = lax.broadcasted_iota(jnp.int32, tail.shape, 1)
    tail = jnp.where(lane < EXPERTS, tail, 0.0) + jnp.where(lane == EXPERTS, gains, 0.0)
    for i, stat in enumerate(stats):
        tail = tail + jnp.where((lane == EXPERTS + 1 + i) & (row == 0), stat, 0.0)
    misc_ref[:, D : D + 128] = tail.astype(BF)


def token_mix(info, pick, mix, mid, x, attn, dbranch, router_t, router_f, dgain, square):
    tok = mid.shape[0]
    operands = [pick, mix, mid, x, attn, dbranch, router_t, router_f, dgain, square]
    return called(
        token_mix_kernel,
        "token_mix",
        [((tok, D), BF), ((D, MISC), BF)],
        info,
        operands,
        micros=1,
    )


def input_grad_kernel(heads, blocks, info_ref, x_ref, gain_ref, dmid_ref, w_ref, *refs):
    grad_refs, out_ref = refs[:blocks], refs[blocks]
    wide = heads * HEAD
    dn1 = 0.0
    for turn in range(blocks):
        g = lax.rem(info_ref[0] + turn, blocks)
        for c in range(3):
            rows = pl.ds(pl.multiple_of(c * blocks * wide + g * wide, HEAD), wide)
            part = grad_refs[turn][c * wide : (c + 1) * wide, :]
            dn1 = dn1 + mm_tn(part, w_ref[rows, :])
    x = x_ref[...].astype(F32)
    r = lax.rsqrt(jnp.mean(x * x, axis=1, keepdims=True) + EPS)
    u = x * r
    scaled = dn1 * gain_ref[...]
    dx = r * (scaled - u * jnp.mean(scaled * u, axis=1, keepdims=True))
    out_ref[...] = (dmid_ref[...] + dx).astype(BF)


def input_grad_rows(heads, info, x, gain, dmid, w_t, grads, deps):
    blocks = len(grads)

    def kernel(*refs):
        input_grad_kernel(heads, blocks, *refs)

    operands = [x, gain, dmid, w_t, *grads]
    return called(
        kernel, "input_grad", [(x.shape, BF)], info, operands, micros=8, deps=deps
    )[0]


def sum_kernel(info_ref, a_ref, out_ref):
    total = a_ref[0].astype(F32)
    for i in range(1, a_ref.shape[0]):
        total = total + a_ref[i].astype(F32)
    out_ref[...] = total.astype(BF)


def sum_parts(info, a, deps):
    return called(sum_kernel, "sum_parts", [(a.shape[1:], BF)], info, [a], micros=3, deps=deps)[0]


def join_kernel(info_ref, *refs):
    found, out_ref, again_ref = refs[:-2], refs[-2], refs[-1]
    total = found[0][:, :MISC].astype(F32)
    for ref in found[1:]:
        total = total + ref[:, :MISC].astype(F32)
    out_ref[:, :MISC] = total.astype(BF)
    cols = found[0].shape[1] - MISC
    for i, ref in enumerate(found):
        out_ref[:, MISC + i * cols : MISC + (i + 1) * cols] = ref[:, MISC:]
    again_ref[...] = out_ref[...]


def join_blocks(info, found, deps):
    rows, cols = found[0].shape
    shape = (rows, MISC + len(found) * (cols - MISC))
    return called(
        join_kernel, "join_blocks", [(shape, BF)] * 2, info, list(found), micros=3, deps=deps
    )


def layout_kernel(heads, groups, info_ref, here_ref, there_ref, w_ref, gain_ref, qkv_ref, out_ref, tail_ref, dgain_ref):
    same = lax.rem(pl.program_id(0), 2) == lax.rem(info_ref[1], 2)
    wide = heads * HEAD
    pieces = jnp.where(same, here_ref[0], there_ref[0])
    out_ref[...] = pieces[:, :D].astype(F32)
    tail_ref[...] = pieces[:, D : D + 128].astype(F32)
    for turn in range(groups):
        g = lax.rem(info_ref[0] - turn + groups, groups)
        for c in range(3):
            at = MISC + (3 * turn + c) * wide
            grad = pieces[:, at : at + wide].astype(F32)
            for g_now in range(groups):
                first = g_now * wide
                cols = min(wide, D - first)
                if cols <= 0:
                    continue
                to = c * D + first

                @pl.when(g == g_now)
                def _():
                    qkv_ref[:, to : to + cols] = grad[:, :cols]

    total = jnp.sum(qkv_ref[...] * w_ref[...].astype(F32), axis=1, keepdims=True)
    dgain_ref[...] = total


def layout(heads, groups, info, here, there, w, gain, deps):
    chips, rows, width = here.shape

    def kernel(*refs):
        layout_kernel(heads, groups, *refs)

    piece_spec = pl.BlockSpec((1, rows, width), lambda e, r: ((e // 2) ^ (r[1] // 2), 0, 0))

    def row_spec(cols):
        return pl.BlockSpec((rows, cols), lambda e, r: (e, 0))

    return called(
        kernel,
        "layout",
        [((D, 3 * D), F32), ((D, D), F32), ((D, 128), F32), ((D, 1), F32)],
        info,
        [here, there, w, gain],
        [piece_spec, piece_spec, row_spec(3 * D), None],
        micros=13,
        grid=(2 * chips,),
        out_specs=[row_spec(3 * D), row_spec(D), row_spec(128), row_spec(1)],
        deps=deps,
    )


def shifted(x, by, count):
    return lax.ppermute(x, "seq", [(i, (i + by) % count) for i in range(count)])


def swap(x, axis):
    return lax.all_to_all(x, axis, split_axis=0, concat_axis=0, tiled=True)


def both_ways(found, step, count):
    up = shifted(found[0], 1, count)
    if 2 * step < count:
        return [up, shifted(found[1], -1, count)]
    return [up]


def body(
    layer_input,
    lengths,
    routes,
    norm1_gain,
    qkv_weight,
    out_weight,
    norm2_gain,
    router_weight,
    frozen_up,
    frozen_down,
    train_up,
    train_down,
    cotangent,
):
    tok = layer_input.shape[1]
    n_seq = lax.axis_size("seq")
    n_exp = lax.axis_size("exp")
    rank = lax.axis_index("seq")
    column = lax.axis_index("exp")
    heads = -(-HEADS // n_seq)
    wide = heads * HEAD
    width = (heads + heads % 2) * HEAD
    local = FROZEN // n_exp
    x_own = layer_input[0]
    g_own = cotangent[0]
    gain1 = norm1_gain[None, :]
    gain2 = norm2_gain[None, :]
    info = jnp.concatenate([jnp.stack([rank, column]).astype(jnp.int32), lengths[0]])

    w_t = qkv_weight.T
    w_parts = jnp.pad(w_t.reshape(3, D, D), ((0, 0), (0, n_seq * wide - D), (0, 0)))
    w_mine = lax.dynamic_slice_in_dim(w_parts, rank * wide, wide, axis=1)
    w_mine = w_mine * jnp.asarray([HEAD**-0.5, 1.0, 1.0], BF)[:, None, None]
    w_mine = jnp.pad(w_mine, ((0, 0), (0, width - wide), (0, 0))).reshape(3 * width, D)
    w_parts = w_parts.reshape(3 * n_seq * wide, D)
    out_groups = jnp.pad(out_weight, ((0, n_seq * wide - D), (0, 0)))
    out_groups = jnp.pad(out_groups.reshape(n_seq, wide, D), ((0, 0), (0, width - wide), (0, 0)))
    feature_head = jnp.arange(D, dtype=jnp.int32) // HEAD
    row_id = jnp.arange(8, dtype=jnp.int32)[None, :] + heads * jnp.arange(n_seq, dtype=jnp.int32)[:, None]
    row_id = jnp.where(jnp.arange(8)[None, :] < heads, row_id, -1)
    head_rows = (row_id[:, :, None] == feature_head[None, None, :]).astype(BF)
    router = jnp.pad(router_weight, ((0, 0), (0, 128 - EXPERTS)))

    pick, g_train, g_frozen = route(info, local, routes[0].T, g_own)
    g_train = swap(g_train, "exp")
    g_frozen = swap(g_frozen, "exp")

    x_now = x_own
    n1_list = []
    state = ()
    sums_own = g_train[:, local * CAP :, :128]
    g_rows = g_train[:, : local * CAP]
    for step in range(n_seq):
        last = step == n_seq - 1
        x_next = None if last else shifted(x_now, 1, n_seq)
        found = attend_step(
            step,
            last,
            info,
            x_now,
            gain1,
            qkv_weight,
            state,
            deps=[g_frozen] if last else [],
            through=[g_rows] if step == n_seq - 2 else [],
        )
        if step == n_seq - 2:
            g_rows = found.pop()
        n1_list.append(found[0])
        state = tuple(found[1:]) if step == 0 else (state[0],) + tuple(found[1:])
        x_now = x_next
    unused_q, attn, lse = state

    mid, branch_squares, rows_train, rows_frozen = token_forward(
        info, attn, x_own, gain2, out_weight, pick
    )
    x_train = swap(rows_train.reshape(n_exp, local, CAP, D), "exp")
    x_frozen = swap(rows_frozen.reshape(n_exp, local, CAP, D), "exp")

    steps = range(1, n_seq // 2 + 1)
    g_steps, x_steps = [[g_rows, g_rows]], []
    for step in steps:
        g_steps.append(both_ways(g_steps[-1], step, n_seq))
    g_steps = g_steps[1:]
    sums = {by: shifted(sums_own, by, n_seq) for by in range(1, n_seq)}
    sum_steps = [
        [sums[step]] + ([sums[n_seq - step]] if 2 * step < n_seq else [])
        for step in steps
    ]

    mix_t, dx_t, do_own, router_t = expert_rows(
        FROZEN, info, x_train, g_train, router, train_up, train_down, []
    )
    dx_t = swap(dx_t, "exp")
    mix_f, dx_f, unused_do, router_f = expert_rows(
        0, info, x_frozen, g_frozen, router, frozen_up, frozen_down, g_steps[0] + [w_mine]
    )
    dx_f = swap(dx_f, "exp")
    x_steps = [both_ways([x_train, x_train], 1, n_seq)]
    for step in steps[1:]:
        x_steps.append(both_ways(x_steps[-1], step, n_seq))

    lse_rows = jnp.pad(lse.reshape(HEADS, tok), ((0, heads * n_seq - HEADS), (0, 0)))
    lse_rows = jnp.pad(lse_rows.reshape(n_seq, heads, tok), ((0, 0), (0, 8 - heads), (0, 0)))
    send, dmid, dbranch, dgain2 = token_back(
        heads,
        n_seq,
        width,
        info,
        pick,
        dx_t,
        dx_f,
        mid,
        g_own,
        gain2,
        out_weight,
        out_groups,
        attn,
        lse_rows,
        head_rows,
        [g for step in g_steps for g in step] + x_steps[0],
    )
    dos = [send[0]] + [shifted(send[step], step, n_seq) for step in range(1, n_seq)]
    qkv_mine, *mix = project_back(info, w_mine, n1_list, [dmid], [mix_t, mix_f])
    mix = swap(jnp.stack(mix, axis=1), "exp")
    gated_steps = [gated(info, router, x_steps[0], g_steps[0], sum_steps[0], [qkv_mine])]
    output, misc = token_mix(
        info, pick, mix, mid, x_own, attn, dbranch, router_t, router_f, dgain2, branch_squares
    )

    dqkv, part = attend_back(heads, info, qkv_mine, misc, n1_list, dos, gated_steps[0])

    parts = swap(part.reshape(n_exp, D // n_exp, part.shape[1]), "exp")
    dqkv_own = [dqkv[0]] + [shifted(dqkv[step], -step, n_seq) for step in range(1, n_seq)]

    for i in range(1, len(x_steps)):
        gated_steps.append(gated(info, router, x_steps[i], g_steps[i], sum_steps[i], [dqkv[0]]))
    xs = [x_train] + [x for step in x_steps for x in step]
    gs = [do_own] + [g for step in gated_steps for g in step]
    tiles = train_up.shape[2] // GRAD_TILE
    grad_parts = [(expert, (0, tiles)) for expert in range(local - 1)]
    grad_parts += [(local - 1, (first, tiles // 2)) for first in (0, tiles // 2)]
    totals = None

    def more_grads(wait, totals, through=()):
        expert, span = grad_parts.pop(0)
        return expert_grads_part(
            expert, span, info, xs, gs, train_up, train_down, totals, wait, through
        )

    totals, done = more_grads([dqkv[0]], totals)
    piece = sum_parts(info, parts, done)

    found = [shifted(piece, step, n_seq) for step in range(1, n_seq)]
    if len(grad_parts) > 1:
        totals, done = more_grads(done, totals)
    found, again = join_blocks(info, [piece] + found, done)
    here = [lax.ppermute(found, "exp", [(i, i ^ m) for i in range(n_exp)]) for m in range(2, n_exp, 2)]
    input_grad = input_grad_rows(heads, info, x_own, gain1, dmid, w_parts, dqkv_own, done)
    while grad_parts:
        totals, (done, again) = more_grads([input_grad], totals, [again])
    here = jnp.stack([again] + here)
    there = lax.ppermute(here, "exp", [(i, i ^ 1) for i in range(n_exp)])
    up_total, down_total = totals
    qkv_total, out_total, tail, dgain1 = layout(
        heads, n_seq, info, here, there, qkv_weight, gain1, [input_grad]
    )
    stat_sums = tail[0, EXPERTS + 1 : EXPERTS + 5]
    stat_roots = jnp.sqrt(stat_sums[:3] / (stat_sums[3] * D))
    return (
        output[None],
        input_grad[None],
        dgain1[:, 0] / norm1_gain,
        qkv_total,
        out_total,
        tail[:, EXPERTS],
        tail[:, :EXPERTS],
        up_total,
        down_total,
        stat_roots,
    )


def solution(mesh):
    return jax.shard_map(
        body,
        mesh=mesh,
        in_specs=(
            P("exp", "seq", None),
            P("exp", None),
            P("exp", "seq", None),
            P(),
            P(),
            P(),
            P(),
            P(),
            P("exp", None, None),
            P("exp", None, None),
            P("exp", None, None),
            P("exp", None, None),
            P("exp", "seq", None),
        ),
        out_specs=(
            P("exp", "seq", None),
            P("exp", "seq", None),
            P(),
            P(),
            P(),
            P(),
            P(),
            P("exp", None, None),
            P("exp", None, None),
            P(),
        ),
        check_vma=False,
    )
```

time: 1570 us -> 505 us (0.32)
  waiting for transfers between devices: 868 us -> 101 us
  matrix products: 299 us -> 0 us
  Pallas kernels: 0 us -> 274 us
  local copies, waits for them, and re-layouts: 181 us -> 28.1 us
  other arithmetic: 125 us -> 10 us
  starting transfers between devices: 19.3 us -> 79.9 us
  blocking collectives: 48.9 us -> 0 us
    psum x2 -> x0, waiting for transfers between devices: 736 us -> none  [the longest x1 561 us: body(): lax.psum(up_grad_local.astype(jnp.bfloat16), 'seq').astype(jnp.float32)]
    dot_general x46 -> x0, matrix products: 299 us -> none  [the longest x4 33.5 us: grad_block(): jnp.einsum('qhd,khd->hqk', attn_grad_heads, value_block, preferred_elemen...]
    pallas_call x0 -> x21, Pallas kernels: none -> 274 us  [called(): return list(call(info, *operands, *through, *deps))]
    ppermute x0 -> x25, waiting for transfers between devices: none -> 87.3 us  [the longest x21 80.8 us: shifted(): return lax.ppermute(x, 'seq', [(i, (i + by) % count) for i in range(count)])]
    reduce_scatter x2 -> x0, waiting for transfers between devices: 57.7 us -> none  [the longest x1 57.7 us: body(): lax.psum_scatter(key_terms.reshape(group_rows, D).astype(jnp.bfloat16), '...]
    all_gather x2 -> x0, waiting for transfers between devices: 54.5 us -> none  [the longest x1 49.2 us: body(): key_rows = lax.all_gather(keys_local, 'seq', axis=0, tiled=True)]
    psum x1 -> x0, blocking collectives: 48.9 us -> none  [body(): lax.psum((qkv_grad_local, out_grad_local, router_grad_local, gain_one_loc...]
    ppermute x0 -> x25, starting transfers between devices: none -> 47.7 us  [the longest x21 44.1 us: shifted(): return lax.ppermute(x, 'seq', [(i, (i + by) % count) for i in range(count)])]
  transfers between devices with their start and end apart: 10 -> 33, of which waited for: 6 -> 9; matrix products, arithmetic and copies ran while one was open for 20% -> 4% of each run, Pallas kernels for 0% -> 48%
where the time goes in v2:
time: 505 us; the launch traced here: 495 us
  Pallas kernels  274 us (54%)
  waiting for transfers between devices  101 us (20%)
  starting transfers between devices  79.9 us (16%)
  local copies, waits for them, and re-layouts  28.1 us (6%)
  other arithmetic  10 us (2%)
    pallas_call x21, Pallas kernels, called(): return list(call(info, *operands, *through, *deps))  274 us
    ppermute x21, waiting for transfers between devices, shifted(): return lax.ppermute(x, 'seq', [(i, (i + by) % count) for i in range(count)])  80.8 us
    ppermute x21, starting transfers between devices, shifted(): return lax.ppermute(x, 'seq', [(i, (i + by) % count) for i in range(count)])  44.1 us
    all_to_all x8, starting transfers between devices, swap(): return lax.all_to_all(x, axis, split_axis=0, concat_axis=0, tiled=True)  32.3 us
    unnamed x47, local copies, waits for them, and re-layouts  15.8 us
    all_to_all x8, waiting for transfers between devices, swap(): return lax.all_to_all(x, axis, split_axis=0, concat_axis=0, tiled=True)  13.4 us
  transfers between devices with their start and end apart: 33, of which 9 were waited for; matrix products, arithmetic and copies ran while one was open for 4% of the time, Pallas kernels for 48%

profile of v2, /device:TPU:0, one launch (start us, length us, event | category | flops | bytes accessed | tf_op | source)
XLA Modules:
  0.0 495.0 jit_solution(18264261108066414996)
XLA Ops:
  0.6 3.1 collective-permute-start
  5.0 5.1 %route.1 = (bf16[1536,512]{1,0:T(8,128)(2,1)}, bf16[8,112,768]{2,1,0:T(8,128)(2,1)}, bf16[8,112,768]{2,1,0:T(8,128)(2,1)}) custom-call(s32[5]{0:T(128)} %pad_add_fusion.info_ref, s32[2,512]{1,0:T(2,128)} %bitcast.52, bf16[512,768]{1,0:T(8,128)(2,1)} %bitcast.49), custom_call_target="tpu_custom_call" | custom-call | flops 6600000000 | tf_op jit(solution)/shard_map/route/pallas_call | solution.py:100
  10.0 3.9 all-to-all-start
  15.1 12.7 %attend_step.4 = (bf16[512,768]{1,0:T(8,128)(2,1)}, bf16[6,512,128]{2,1,0:T(8,128)(2,1)}, f32[6,2,512]{2,1,0:T(2,128)}, f32[6,2,512]{2,1,0:T(2,128)}, f32[768,512]{1,0:T(8,128)}) custom-call(s32[5]{0:T(128)} %pad_add_fusion.info_ref, bf16[512,768]{1,0:T(8,128)(2,1)} %bitcast.40, f32[1,768]{1,0:T(1,128)} %broadcast_in_dim.30.refs_1_.refs_3_, ...), custom_call_target="tpu_custom_call" | custom-call | flops 14300000256 | tf_op jit(solution)/shard_map/attend_step/pallas_call | solution.py:100
  29.4 5.6 %attend_step.5 = (bf16[512,768]{1,0:T(8,128)(2,1)}, f32[6,2,512]{2,1,0:T(2,128)}, f32[6,2,512]{2,1,0:T(2,128)}, f32[768,512]{1,0:T(8,128)}) custom-call(s32[5]{0:T(128)} %pad_add_fusion.info_ref, bf16[512,768]{1,0:T(8,128)(2,1)} %copy-done.17, f32[1,768]{1,0:T(1,128)} %broadcast_in_dim.30.refs_1_.refs_3_, bf16[768,2304]{1,0:T(8,128)(2,1)} %refs_2_.9, ...), custom_call_target="tpu_custom_call" | custom-call | flops 14300000256 | tf_op jit(solution)/shard_map/attend_step/pallas_call | solution.py:100
  35.0 4.2 all-to-all-start.1
  40.4 9.3 %collective-permute-done.1.refs_0_ = bf16[512,768]{1,0:T(8,128)(2,1)} collective-permute-done((bf16[512,768]{1,0:T(8,128)(2,1)S(1)}, bf16[512,768]{1,0:T(8,128)(2,1)}, u32[]{:S(2)}, u32[]{:S(2)}) %collective-permute-start.1) | collective-permute-done | bytes 786464 | tf_op jit(solution)/shard_map/ppermute | solution.py:984
  49.7 5.5 %attend_step.6 = (bf16[512,768]{1,0:T(8,128)(2,1)}, f32[6,2,512]{2,1,0:T(2,128)}, f32[6,2,512]{2,1,0:T(2,128)}, f32[768,512]{1,0:T(8,128)}, bf16[8,96,768]{2,1,0:T(8,128)(2,1)}) custom-call(s32[5]{0:T(128)} %pad_add_fusion.info_ref, bf16[512,768]{1,0:T(8,128)(2,1)} %collective-permute-done.1.refs_0_, ...), custom_call_target="tpu_custom_call", output_to_operand_aliasing={{4}: (10, {})} | custom-call | flops 14300000256 | tf_op jit(solution)/shard_map/attend_step/pallas_call | solution.py:100
  55.2 11.2 %collective-permute-start.4 = (bf16[8,96,768]{2,1,0:T(8,128)(2,1)}, bf16[8,96,768]{2,1,0:T(8,128)(2,1)}, u32[]{:S(2)}, u32[]{:S(2)}) collective-permute-start(bf16[8,96,768]{2,1,0:T(8,128)(2,1)} %get-tuple-element.96), channel_id=1, source_target_pairs={{0,24},{8,0},{16,8},{24,16},{1,25},{9,1},{17,9},{25,17},{2,26},{10... | collective-permute-start | bytes 3538952 | tf_op jit(solution)/shard_map/ppermute | solution.py:984
  66.6 5.6 %collective-permute-done.2.refs_0_ = bf16[512,768]{1,0:T(8,128)(2,1)S(1)} collective-permute-done((bf16[512,768]{1,0:T(8,128)(2,1)}, bf16[512,768]{1,0:T(8,128)(2,1)S(1)}, u32[]{:S(2)}, u32[]{:S(2)}) %collective-permute-start.2) | collective-permute-done | bytes 786464 | tf_op jit(solution)/shard_map/ppermute | solution.py:984
  73.1 5.4 %attend_step.7 = (bf16[512,768]{1,0:T(8,128)(2,1)}, bf16[512,768]{1,0:T(8,128)(2,1)}, f32[6,2,512]{2,1,0:T(2,128)}) custom-call(s32[5]{0:T(128)} %pad_add_fusion.info_ref, bf16[512,768]{1,0:T(8,128)(2,1)} %copy-done.18, f32[1,768]{1,0:T(1,128)} %broadcast_in_dim.30.refs_1_.refs_3_, bf16[768,2304]{1,0:T(8,128)(2,1)} %refs_2_.9, bf16[768,2304]{1,0:T(8,128)(2,1)} %refs_2_.9, ...), custom_call_target="tpu_custom_call" | custom-call | flops 14300000256 | tf_op jit(solution)/shard_map/attend_step/pallas_call | solution.py:100
  78.5 6.6 %token_forward.1 = (f32[512,768]{1,0:T(8,128)}, f32[1,768]{1,0:T(1,128)}, bf16[768,768]{1,0:T(8,128)(2,1)}, bf16[768,768]{1,0:T(8,128)(2,1)}) custom-call(s32[5]{0:T(128)} %pad_add_fusion.info_ref, bf16[512,768]{1,0:T(8,128)(2,1)} %get-tuple-element.92.refs_0_.refs_8_.refs_4_, bf16[512,768]{1,0:T(8,128)(2,1)} %bitcast.41, ...), custom_call_target="tpu_custom_call" | custom-call | flops 6600000000 | tf_op jit(solution)/shard_map/token_forward/pallas_call | solution.py:100
  85.1 4.2 all-to-all-start.3
  89.4 4.5 copy.35
  98.8 22.9 %collective-permute-done.3.refs_6_.refs_11_.refs_3_ = bf16[8,96,768]{2,1,0:T(8,128)(2,1)} collective-permute-done((bf16[8,96,768]{2,1,0:T(8,128)(2,1)}, bf16[8,96,768]{2,1,0:T(8,128)(2,1)}, u32[]{:S(2)}, u32[]{:S(2)}) %collective-permute-start.3) | collective-permute-done | bytes 1179680 | tf_op jit(solution)/shard_map/ppermute | solution.py:984
  121.6 3.6 all-to-all-start.2
  125.2 24.1 %expert_rows.3 = (bf16[8,2,48,768]{3,2,1,0:T(8,128)(2,1)}, bf16[8,2,48,768]{3,2,1,0:T(8,128)(2,1)}, bf16[8,2,48,768]{3,2,1,0:T(8,128)(2,1)}, f32[128,768]{1,0:T(8,128)}) custom-call(s32[5]{0:T(128)} %pad_add_fusion.info_ref, bf16[8,2,48,768]{3,2,1,0:T(8,128)(2,1)} %all-to-all-done.3.refs_0_, bf16[8,112,768]{2,1,0:T(8,128)(2,1)} %copy-done.5, ...), custom_call_target="tpu_custom_call" | custom-call | flops 25300000768 | tf_op jit(solution)/shard_map/expert_rows/pallas_call | solution.py:100
  149.4 4.3 all-to-all-start.5
  153.6 3.9 collective-permute-start.7
  157.5 3.0 collective-permute-start.6
  160.5 23.9 %expert_rows.2 = (bf16[8,2,48,768]{3,2,1,0:T(8,128)(2,1)}, bf16[8,2,48,768]{3,2,1,0:T(8,128)(2,1)}, bf16[8,2,48,768]{3,2,1,0:T(8,128)(2,1)}, f32[128,768]{1,0:T(8,128)}) custom-call(s32[5]{0:T(128)} %pad_add_fusion.info_ref, bf16[8,2,48,768]{3,2,1,0:T(8,128)(2,1)} %copy-done.9, bf16[8,112,768]{2,1,0:T(8,128)(2,1)} %copy-done.2, ...), custom_call_target="tpu_custom_call" | custom-call | flops 25300000768 | tf_op jit(solution)/shard_map/expert_rows/pallas_call | solution.py:100
  184.5 4.4 all-to-all-start.4
  192.3 13.4 %all-to-all-done.4.refs_1_ = bf16[8,2,48,768]{3,2,1,0:T(8,128)(2,1)} async-done(((bf16[8,2,48,768]{3,2,1,0:T(8,128)(2,1)}), bf16[8,2,48,768]{3,2,1,0:T(8,128)(2,1)}, u32[]{:S(2)}, u32[]{:S(2)}) %all-to-all-start.4) | async-done | bytes 1179680 | tf_op jit(solution)/shard_map/all_to_all | solution.py:988
  205.7 9.7 %collective-permute-done.6.refs_14_.refs_1_.refs_3_ = bf16[8,2,48,768]{3,2,1,0:T(8,128)(2,1)} collective-permute-done((bf16[8,2,48,768]{3,2,1,0:T(8,128)(2,1)S(1)}, bf16[8,2,48,768]{3,2,1,0:T(8,128)(2,1)}, u32[]{:S(2)}, u32[]{:S(2)}) %collective-permute-start.6) | collective-permute-done | bytes 1179680 | tf_op jit(solution)/shard_map/ppermute | solution.py:984
  215.3 11.8 %token_back.1 = (bf16[2,272,256]{2,1,0:T(8,128)(2,1)}, bf16[2,272,256]{2,1,0:T(8,128)(2,1)}, bf16[2,272,256]{2,1,0:T(8,128)(2,1)}, bf16[2,272,256]{2,1,0:T(8,128...) custom-call(s32[5]{0:T(128)} %pad_add_fusion.info_ref, ...), custom_call_target="tpu_custom_call" | custom-call | flops 11000000512 | tf_op jit(solution)/shard_map/token_back/pallas_call | solution.py:100
  227.1 7.2 %project_back.1 = (bf16[2048,768]{1,0:T(8,128)(2,1)}, bf16[8,2,48,768]{3,2,1,0:T(8,128)(2,1)}, bf16[8,2,48,768]{3,2,1,0:T(8,128)(2,1)}) custom-call(s32[5]{0:T(128)} %pad_add_fusion.info_ref, bf16[768,768]{1,0:T(8,128)(2,1)} %bitcast.31, bf16[512,768]{1,0:T(8,128)(2,1)} %get-tuple-element.76.refs_1_.refs_2_, ...), custom_call_target="tpu_custom_call", output_to_operand_aliasing={{1}: (6, {}), {2}: (7, {})} | custom-call | flops 1100000000 | tf_op jit(solution)/shard_map/project_back/pallas_call | solution.py:100
  234.3 3.2 pad_maximum_fusion.1
  237.5 3.9 all-to-all-start.6
  241.5 3.7 collective-permute-start.10
  248.8 15.5 %collective-permute-done.12.refs_6_ = bf16[8,16,128]{2,1,0:T(8,128)(2,1)S(1)} collective-permute-done((bf16[8,16,128]{2,1,0:T(8,128)(2,1)}, bf16[8,16,128]{2,1,0:T(8,128)(2,1)S(1)}, u32[]{:S(2)}, u32[]{:S(2)}) %collective-permute-start.12) | collective-permute-done | bytes 32800 | tf_op jit(solution)/shard_map/ppermute | solution.py:984
  264.2 6.4 %collective-permute-start.17 = (bf16[8,16,128]{2,1,0:T(8,128)(2,1)}, bf16[8,16,128]{2,1,0:T(8,128)(2,1)}, u32[]{:S(2)}, u32[]{:S(2)}) collective-permute-start(bf16[8,16,128]{2,1,0:T(8,128)(2,1)} %slice.30), channel_id=1, source_target_pairs={{0,16},{8,24},{16,0},{24,8},{1,17},{9,25},{17,1},{25,9},{2,18},{10... | collective-permute-start | bytes 98312 | tf_op jit(solution)/shard_map/ppermute | solution.py:984
  271.6 5.8 %gated.2 = (bf16[8,2,48,768]{3,2,1,0:T(8,128)(2,1)}, bf16[8,2,48,768]{3,2,1,0:T(8,128)(2,1)}) custom-call(s32[5]{0:T(128)} %pad_add_fusion.info_ref, bf16[768,128]{1,0:T(8,128)(2,1)} %pad.17.refs_3_.refs_0_, bf16[8,2,48,768]{3,2,1,0:T(8,128)(2,1)} %collective-permute-done.6.refs_14_.refs_1_.refs_3_, ...), custom_call_target="tpu_custom_call" | custom-call | flops 1100000000 | tf_op jit(solution)/shard_map/gated/pallas_call | solution.py:100
  278.9 7.4 %token_mix.1 = (bf16[512,768]{1,0:T(8,128)(2,1)}, bf16[768,896]{1,0:T(8,128)(2,1)}) custom-call(s32[5]{0:T(128)} %pad_add_fusion.info_ref, bf16[1536,512]{1,0:T(8,128)(2,1)} %get-tuple-element.75.refs_4_.refs_0_, bf16[8,2,2,48,768]{4,3,2,1,0:T(8,128)(2,1)} %copy-done, f32[512,768]{1,0:T(8,128)} %get-tuple-element.100.refs_3_.refs_2_, ...), custom_call_target="tpu_custom_call" | custom-call | flops 1100000000 | tf_op jit(solution)/shard_map/token_mix/pallas_call | solution.py:100
  286.3 32.7 %attend_back.1 = (bf16[576,512]{1,0:T(8,128)(2,1)}, bf16[576,512]{1,0:T(8,128)(2,1)}, bf16[576,512]{1,0:T(8,128)(2,1)}, bf16[576,512]{1,0:T(8,128)(2,1)}, bf16[768,1472]{1,0:T(8,128)(2,1)}) custom-call(s32[5]{0:T(128)} %pad_add_fusion.info_ref, bf16[2048,768]{1,0:T(8,128)(2,1)} %get-tuple-element.111.refs_7_.refs_0_, ...), custom_call_target="tpu_custom_call" | custom-call | flops 35200000000 | tf_op jit(solution)/shard_map/attend_back/pallas_call | solution.py:100
  319.0 3.8 all-to-all-start.7
  322.8 2.9 collective-permute-start.13
  325.7 2.0 collective-permute-start.15
  328.7 4.4 gated.3.refs_9_
  333.1 41.3 %expert_grads.3 = (f32[2,768,3072]{2,1,0:T(8,128)}, f32[2,3072,768]{2,1,0:T(8,128)}, f32[8,128]{1,0:T(8,128)}) custom-call(s32[5]{0:T(128)} %pad_add_fusion.info_ref, bf16[2,768,3072]{2,1,0:T(8,128)(2,1)} %refs_0_.5, bf16[2,3072,768]{2,1,0:T(8,128)(2,1)} %refs_1_.5, bf16[8,2,48,768]{3,2,1,0:T(8,128)(2,1)} %copy-done.9, ...), custom_call_target="tpu_custom_call" | custom-call | flops 39600001024 | tf_op jit(solution)/shard_map/expert_grads/pallas_call | solution.py:100
  374.4 23.6 %expert_grads.4 = (f32[2,768,3072]{2,1,0:T(8,128)}, f32[2,3072,768]{2,1,0:T(8,128)}, f32[8,128]{1,0:T(8,128)}) custom-call(s32[5]{0:T(128)} %pad_add_fusion.info_ref, bf16[2,768,3072]{2,1,0:T(8,128)(2,1)} %refs_0_.5, bf16[2,3072,768]{2,1,0:T(8,128)(2,1)} %refs_1_.5, ...), custom_call_target="tpu_custom_call", output_to_operand_aliasing={{0}: (11, {}), {1}: (12, {})} | custom-call | flops 19800000512 | tf_op jit(solution)/shard_map/expert_grads/pallas_call | solution.py:100
  399.5 3.4 sum_parts.1.refs_0_
  405.8 7.9 %input_grad.1.refs_13_.refs_4_ = bf16[512,768]{1,0:T(8,128)(2,1)} custom-call(s32[5]{0:T(128)} %pad_add_fusion.info_ref, bf16[512,768]{1,0:T(8,128)(2,1)} %bitcast.43, f32[1,768]{1,0:T(1,128)} %broadcast_in_dim.30.refs_1_.refs_3_, f32[512,768]{1,0:T(8,128)} %get-tuple-element.102.refs_7_.refs_2_, bf16[2304,768]{1,0:T(8,128)(2,1)} %bitcast.29, ...), custom_call_target="tpu_custom_call" | custom-call | flops 8800000000 | tf_op jit(solution)/shard_map/input_grad/pallas_call | solution.py:100
  413.7 17.8 %collective-permute-done.19.refs_2_ = bf16[96,1472]{1,0:T(8,128)(2,1)S(1)} collective-permute-done((bf16[96,1472]{1,0:T(8,128)(2,1)}, bf16[96,1472]{1,0:T(8,128)(2,1)S(1)}, u32[]{:S(2)}, u32[]{:S(2)}) %collective-permute-start.19) | collective-permute-done | bytes 282656 | tf_op jit(solution)/shard_map/ppermute | solution.py:984
  433.0 3.2 join_blocks.1
  436.2 2.6 collective-permute-start.23
  439.6 23.4 %expert_grads.5 = (f32[2,768,3072]{2,1,0:T(8,128)}, f32[2,3072,768]{2,1,0:T(8,128)}, f32[8,128]{1,0:T(8,128)}, bf16[96,3200]{1,0:T(8,128)(2,1)}) custom-call(s32[5]{0:T(128)} %pad_add_fusion.info_ref, bf16[2,768,3072]{2,1,0:T(8,128)(2,1)} %refs_0_.5, bf16[2,3072,768]{2,1,0:T(8,128)(2,1)} %refs_1_.5, ...), custom_call_target="tpu_custom_call", output_to_operand_aliasing={{0}: (11, {}), {1}: (12, {}), {3}: (13, {})} | custom-call | flops 19800000512 | tf_op jit(solution)/shard_map/expert_grads/pallas_call | solution.py:100
  466.5 4.7 collective-permute-done.24.refs_1_
  472.6 13.5 %layout.1 = (f32[768,2304]{1,0:T(8,128)}, f32[768,768]{1,0:T(8,128)}, f32[768,128]{1,0:T(8,128)}, f32[768,1]{1,0:T(8,128)}) custom-call(s32[5]{0:T(128)} %pad_add_fusion.info_ref, bf16[4,96,3200]{2,1,0:T(8,128)(2,1)} %copy-done.3, bf16[4,96,3200]{2,1,0:T(8,128)(2,1)} %copy-done.16, bf16[768,2304]{1,0:T(8,128)(2,1)} %refs_2_.9, ...), custom_call_target="tpu_custom_call" | custom-call | flops 14300000256 | tf_op jit(solution)/shard_map/layout/pallas_call | solution.py:100
  (109 shorter events, 41.3 us)
Async XLA Ops:
  0.6 27.1 %collective-permute-start = (bf16[512,768]{1,0:T(8,128)(2,1)}, bf16[512,768]{1,0:T(8,128)(2,1)S(1)}, u32[]{:S(2)}, u32[]{:S(2)}) collective-permute-start(bf16[512,768]{1,0:T(8,128)(2,1)} %bitcast.39), channel_id=1, source_target_pairs={{0,8},{8,16},{16,24},{24,0},{1,9},{9,17},{17,25},{25,1},{2,10},{10... | collective-permute-start | bytes 2359304 | tf_op jit(solution)/shard_map/ppermute | solution.py:984
  10.0 3.9 copy-start.12
  10.0 4.5 copy-start.14
  10.0 25.0 %all-to-all-start = ((bf16[8,112,768]{2,1,0:T(8,128)(2,1)}), bf16[8,112,768]{2,1,0:T(8,128)(2,1)S(1)}, u32[]{:S(2)}, u32[]{:S(2)}) async-start(bf16[8,112,768]{2,1,0:T(8,128)(2,1)} %get-tuple-element.85), calls=%async_computation | async-start | bytes 2752512 | tf_op jit(solution)/shard_map/all_to_all | solution.py:988
  27.8 1.6 copy-start.17
  27.8 21.9 %collective-permute-start.1 = (bf16[512,768]{1,0:T(8,128)(2,1)S(1)}, bf16[512,768]{1,0:T(8,128)(2,1)}, u32[]{:S(2)}, u32[]{:S(2)}) collective-permute-start(bf16[512,768]{1,0:T(8,128)(2,1)S(1)} %collective-permute-done.refs_0_), channel_id=1, source_target_pairs={{0,8},{8,16},{16,24},{24,0},{1,9},{9,17},{17,25},{25,1},{2,10},{10... | collective-permute-start | bytes 2359304 | tf_op jit(solution)/shard_map/ppermute | solution.py:984
  35.0 5.4 %copy-start.2 = (bf16[8,112,768]{2,1,0:T(8,128)(2,1)}, bf16[8,112,768]{2,1,0:T(8,128)(2,1)S(1)}, u32[]{:S(2)}) copy-start(bf16[8,112,768]{2,1,0:T(8,128)(2,1)S(1)} %all-to-all-done.refs_1_.refs_2_) | copy-start | bytes 4128772
  35.0 31.6 %all-to-all-start.1 = ((bf16[8,112,768]{2,1,0:T(8,128)(2,1)}), bf16[8,112,768]{2,1,0:T(8,128)(2,1)S(1)}, u32[]{:S(2)}, u32[]{:S(2)}) async-start(bf16[8,112,768]{2,1,0:T(8,128)(2,1)} %get-tuple-element.90), calls=%async_computation.1 | async-start | bytes 2752512 | tf_op jit(solution)/shard_map/all_to_all | solution.py:988
  49.7 22.5 %collective-permute-start.2 = (bf16[512,768]{1,0:T(8,128)(2,1)}, bf16[512,768]{1,0:T(8,128)(2,1)S(1)}, u32[]{:S(2)}, u32[]{:S(2)}) collective-permute-start(bf16[512,768]{1,0:T(8,128)(2,1)} %collective-permute-done.1.refs_0_), channel_id=1, source_target_pairs={{0,8},{8,16},{16,24},{24,0},{1,9},{9,17},{17,25},{25,1},{2,10},{10... | collective-permute-start | bytes 2359304 | tf_op jit(solution)/shard_map/ppermute | solution.py:984
  55.2 70.0 %collective-permute-start.4 = (bf16[8,96,768]{2,1,0:T(8,128)(2,1)}, bf16[8,96,768]{2,1,0:T(8,128)(2,1)}, u32[]{:S(2)}, u32[]{:S(2)}) collective-permute-start(bf16[8,96,768]{2,1,0:T(8,128)(2,1)} %get-tuple-element.96), channel_id=1, source_target_pairs={{0,24},{8,0},{16,8},{24,16},{1,25},{9,1},{17,9},{25,17},{2,26},{10... | collective-permute-start | bytes 3538952 | tf_op jit(solution)/shard_map/ppermute | solution.py:984
  66.4 55.2 %collective-permute-start.3 = (bf16[8,96,768]{2,1,0:T(8,128)(2,1)}, bf16[8,96,768]{2,1,0:T(8,128)(2,1)}, u32[]{:S(2)}, u32[]{:S(2)}) collective-permute-start(bf16[8,96,768]{2,1,0:T(8,128)(2,1)} %get-tuple-element.96), channel_id=1, source_target_pairs={{0,8},{8,16},{16,24},{24,0},{1,9},{9,17},{17,25},{25,1},{2,10},{10... | collective-permute-start | bytes 3538952 | tf_op jit(solution)/shard_map/ppermute | solution.py:984
  66.6 5.7 %copy-start.5 = (bf16[8,112,768]{2,1,0:T(8,128)(2,1)}, bf16[8,112,768]{2,1,0:T(8,128)(2,1)S(1)}, u32[]{:S(2)}) copy-start(bf16[8,112,768]{2,1,0:T(8,128)(2,1)S(1)} %all-to-all-done.1.refs_9_.refs_1_.refs_2_) | copy-start | bytes 4128772
  85.1 36.5 %all-to-all-start.3 = ((bf16[8,2,48,768]{3,2,1,0:T(8,128)(2,1)}), bf16[8,2,48,768]{3,2,1,0:T(8,128)(2,1)}, u32[]{:S(2)}, u32[]{:S(2)}) async-start(bf16[8,2,48,768]{3,2,1,0:T(8,128)(2,1)} %bitcast.38), calls=%async_computation.3 | async-start | bytes 2359296 | tf_op jit(solution)/shard_map/all_to_all | solution.py:988
  89.3 8.0 %copy-start.15 = (bf16[3]{0:T(256)(128)(2,1)S(1)}, bf16[3]{0:T(256)(128)(2,1)}, u32[]{:S(2)}) copy-start(bf16[3]{0:T(256)(128)(2,1)} %constant.44.clone) | copy-start | bytes 22
  93.9 4.9 copy-start.1
  121.6 70.7 %collective-permute-start.5 = (bf16[8,96,768]{2,1,0:T(8,128)(2,1)}, bf16[8,96,768]{2,1,0:T(8,128)(2,1)S(1)}, u32[]{:S(2)}, u32[]{:S(2)}) collective-permute-start(bf16[8,96,768]{2,1,0:T(8,128)(2,1)} %collective-permute-done.3.refs_6_.refs_11_.refs_3_), channel_id=1, source_target_pairs={{0,8},{8,16},{16,24},{24,0},{1,9},{9,17},{17,25},{25,1},{2,10},{10... | collective-permute-start | bytes 3538952 | tf_op jit(solution)/shard_map/ppermute | solution.py:984
  121.6 27.7 %all-to-all-start.2 = ((bf16[8,2,48,768]{3,2,1,0:T(8,128)(2,1)}), bf16[8,2,48,768]{3,2,1,0:T(8,128)(2,1)S(1)}, u32[]{:S(2)}, u32[]{:S(2)}) async-start(bf16[8,2,48,768]{3,2,1,0:T(8,128)(2,1)} %bitcast.37), calls=%async_computation.2 | async-start | bytes 2359296 | tf_op jit(solution)/shard_map/all_to_all | solution.py:988
  149.4 11.1 %copy-start.9 = (bf16[8,2,48,768]{3,2,1,0:T(8,128)(2,1)}, bf16[8,2,48,768]{3,2,1,0:T(8,128)(2,1)S(1)}, u32[]{:S(2)}) copy-start(bf16[8,2,48,768]{3,2,1,0:T(8,128)(2,1)S(1)} %all-to-all-done.2.refs_0_.refs_2_) | copy-start | bytes 3538948
  149.4 35.1 %all-to-all-start.5 = ((bf16[8,2,48,768]{3,2,1,0:T(8,128)(2,1)}), bf16[8,2,48,768]{3,2,1,0:T(8,128)(2,1)}, u32[]{:S(2)}, u32[]{:S(2)}) async-start(bf16[8,2,48,768]{3,2,1,0:T(8,128)(2,1)} %get-tuple-element.99), calls=%async_computation.5 | async-start | bytes 2359296 | tf_op jit(solution)/shard_map/all_to_all | solution.py:988
  153.6 52.0 %collective-permute-start.7 = (bf16[8,2,48,768]{3,2,1,0:T(8,128)(2,1)S(1)}, bf16[8,2,48,768]{3,2,1,0:T(8,128)(2,1)}, u32[]{:S(2)}, u32[]{:S(2)}) collective-permute-start(bf16[8,2,48,768]{3,2,1,0:T(8,128)(2,1)S(1)} %all-to-all-done.2.refs_0_.refs_2_), channel_id=1, source_target_pairs={{0,24},{8,0},{16,8},{24,16},{1,25},{9,1},{17,9},{25,17},{2,26},{10... | collective-permute-start | bytes 3538952 | tf_op jit(solution)/shard_map/ppermute | solution.py:984
  157.5 57.8 %collective-permute-start.6 = (bf16[8,2,48,768]{3,2,1,0:T(8,128)(2,1)S(1)}, bf16[8,2,48,768]{3,2,1,0:T(8,128)(2,1)}, u32[]{:S(2)}, u32[]{:S(2)}) collective-permute-start(bf16[8,2,48,768]{3,2,1,0:T(8,128)(2,1)S(1)} %all-to-all-done.2.refs_0_.refs_2_), channel_id=1, source_target_pairs={{0,8},{8,16},{16,24},{24,0},{1,9},{9,17},{17,25},{25,1},{2,10},{10... | collective-permute-start | bytes 3538952 | tf_op jit(solution)/shard_map/ppermute | solution.py:984
  184.4 4.4 copy-start.8
  184.5 21.2 %all-to-all-start.4 = ((bf16[8,2,48,768]{3,2,1,0:T(8,128)(2,1)}), bf16[8,2,48,768]{3,2,1,0:T(8,128)(2,1)}, u32[]{:S(2)}, u32[]{:S(2)}) async-start(bf16[8,2,48,768]{3,2,1,0:T(8,128)(2,1)} %get-tuple-element.98), calls=%async_computation.4 | async-start | bytes 2359296 | tf_op jit(solution)/shard_map/all_to_all | solution.py:988
  192.3 23.0 %copy-start.6 = (bf16[8,96,768]{2,1,0:T(8,128)(2,1)}, bf16[8,96,768]{2,1,0:T(8,128)(2,1)S(1)}, u32[]{:S(2)}) copy-start(bf16[8,96,768]{2,1,0:T(8,128)(2,1)S(1)} %collective-permute-done.5.refs_13_.refs_2_) | copy-start | bytes 3538948
  237.5 39.9 %all-to-all-start.6 = ((bf16[8,2,2,48,768]{4,3,2,1,0:T(8,128)(2,1)}), bf16[8,2,2,48,768]{4,3,2,1,0:T(8,128)(2,1)S(1)}, u32[]{:S(2)}, u32[]{:S(2)}) async-start(bf16[8,2,2,48,768]{4,3,2,1,0:T(8,128)(2,1)} %pad_maximum_fusion.1), calls=%async_computation.6 | async-start | bytes 4718592 | tf_op jit(solution)/shard_map/all_to_all | solution.py:988
  241.4 44.9 %collective-permute-start.8 = (bf16[2,272,256]{2,1,0:T(8,128)(2,1)}, bf16[2,272,256]{2,1,0:T(8,128)(2,1)}, u32[]{:S(2)}, u32[]{:S(2)}) collective-permute-start(bf16[2,272,256]{2,1,0:T(8,128)(2,1)} %get-tuple-element.114), channel_id=1, source_target_pairs={{0,8},{8,16},{16,24},{24,0},{1,9},{9,17},{17,25},{25,1},{2,10},{10... | collective-permute-start | bytes 835592 | tf_op jit(solution)/shard_map/ppermute | solution.py:984
  241.4 44.9 %collective-permute-start.9 = (bf16[2,272,256]{2,1,0:T(8,128)(2,1)}, bf16[2,272,256]{2,1,0:T(8,128)(2,1)}, u32[]{:S(2)}, u32[]{:S(2)}) collective-permute-start(bf16[2,272,256]{2,1,0:T(8,128)(2,1)} %get-tuple-element.115), channel_id=1, source_target_pairs={{0,16},{8,24},{16,0},{24,8},{1,17},{9,25},{17,1},{25,9},{2,18},{10... | collective-permute-start | bytes 835592 | tf_op jit(solution)/shard_map/ppermute | solution.py:984
  241.5 44.8 %collective-permute-start.10 = (bf16[2,272,256]{2,1,0:T(8,128)(2,1)}, bf16[2,272,256]{2,1,0:T(8,128)(2,1)}, u32[]{:S(2)}, u32[]{:S(2)}) collective-permute-start(bf16[2,272,256]{2,1,0:T(8,128)(2,1)} %get-tuple-element.116), channel_id=1, source_target_pairs={{0,24},{8,0},{16,8},{24,16},{1,25},{9,1},{17,9},{25,17},{2,26},{10... | collective-permute-start | bytes 835592 | tf_op jit(solution)/shard_map/ppermute | solution.py:984
  246.6 17.6 %collective-permute-start.12 = (bf16[8,16,128]{2,1,0:T(8,128)(2,1)}, bf16[8,16,128]{2,1,0:T(8,128)(2,1)S(1)}, u32[]{:S(2)}, u32[]{:S(2)}) collective-permute-start(bf16[8,16,128]{2,1,0:T(8,128)(2,1)} %slice.30), channel_id=1, source_target_pairs={{0,24},{8,0},{16,8},{24,16},{1,25},{9,1},{17,9},{25,17},{2,26},{10... | collective-permute-start | bytes 98312 | tf_op jit(solution)/shard_map/ppermute | solution.py:984
  247.2 23.4 %collective-permute-start.11 = (bf16[8,16,128]{2,1,0:T(8,128)(2,1)}, bf16[8,16,128]{2,1,0:T(8,128)(2,1)S(1)}, u32[]{:S(2)}, u32[]{:S(2)}) collective-permute-start(bf16[8,16,128]{2,1,0:T(8,128)(2,1)} %slice.30), channel_id=1, source_target_pairs={{0,8},{8,16},{16,24},{24,0},{1,9},{9,17},{17,25},{25,1},{2,10},{10... | collective-permute-start | bytes 98312 | tf_op jit(solution)/shard_map/ppermute | solution.py:984
  264.2 7.4 %copy-start.10 = (bf16[8,16,128]{2,1,0:T(8,128)(2,1)}, bf16[8,16,128]{2,1,0:T(8,128)(2,1)S(1)}, u32[]{:S(2)}) copy-start(bf16[8,16,128]{2,1,0:T(8,128)(2,1)S(1)} %collective-permute-done.12.refs_6_) | copy-start | bytes 98308
  264.2 63.5 %collective-permute-start.17 = (bf16[8,16,128]{2,1,0:T(8,128)(2,1)}, bf16[8,16,128]{2,1,0:T(8,128)(2,1)}, u32[]{:S(2)}, u32[]{:S(2)}) collective-permute-start(bf16[8,16,128]{2,1,0:T(8,128)(2,1)} %slice.30), channel_id=1, source_target_pairs={{0,16},{8,24},{16,0},{24,8},{1,17},{9,25},{17,1},{25,9},{2,18},{10... | collective-permute-start | bytes 98312 | tf_op jit(solution)/shard_map/ppermute | solution.py:984
  270.6 57.1 %collective-permute-start.16 = (bf16[8,2,48,768]{3,2,1,0:T(8,128)(2,1)}, bf16[8,2,48,768]{3,2,1,0:T(8,128)(2,1)S(1)}, u32[]{:S(2)}, u32[]{:S(2)}) collective-permute-start(bf16[8,2,48,768]{3,2,1,0:T(8,128)(2,1)} %collective-permute-done.6.refs_14_.refs_1_.refs_3_), channel_id=1, source_target_pairs={{0,8},{8,16},{16,24},{24,0},{1,9},{9,17},{17,25},{25,1},{2,10},{10... | collective-permute-start | bytes 3538952 | tf_op jit(solution)/shard_map/ppermute | solution.py:984
  319.0 79.1 %all-to-all-start.7 = ((bf16[8,96,1472]{2,1,0:T(8,128)(2,1)}), bf16[8,96,1472]{2,1,0:T(8,128)(2,1)S(1)}, u32[]{:S(2)}, u32[]{:S(2)}) async-start(bf16[8,96,1472]{2,1,0:T(8,128)(2,1)} %bitcast.34), calls=%async_computation.7 | async-start | bytes 4718592 | tf_op jit(solution)/shard_map/all_to_all | solution.py:988
  322.8 83.0 %collective-permute-start.13 = (bf16[576,512]{1,0:T(8,128)(2,1)}, bf16[576,512]{1,0:T(8,128)(2,1)}, u32[]{:S(2)}, u32[]{:S(2)}) collective-permute-start(bf16[576,512]{1,0:T(8,128)(2,1)} %get-tuple-element.120), channel_id=1, source_target_pairs={{0,24},{8,0},{16,8},{24,16},{1,25},{9,1},{17,9},{25,17},{2,26},{10... | collective-permute-start | bytes 1769480 | tf_op jit(solution)/shard_map/ppermute | solution.py:984
  325.7 80.1 %collective-permute-start.14 = (bf16[576,512]{1,0:T(8,128)(2,1)}, bf16[576,512]{1,0:T(8,128)(2,1)}, u32[]{:S(2)}, u32[]{:S(2)}) collective-permute-start(bf16[576,512]{1,0:T(8,128)(2,1)} %get-tuple-element.121), channel_id=1, source_target_pairs={{0,16},{8,24},{16,0},{24,8},{1,17},{9,25},{17,1},{25,9},{2,18},{10... | collective-permute-start | bytes 1769480 | tf_op jit(solution)/shard_map/ppermute | solution.py:984
  325.7 80.1 %collective-permute-start.15 = (bf16[576,512]{1,0:T(8,128)(2,1)}, bf16[576,512]{1,0:T(8,128)(2,1)}, u32[]{:S(2)}, u32[]{:S(2)}) collective-permute-start(bf16[576,512]{1,0:T(8,128)(2,1)} %get-tuple-element.122), channel_id=1, source_target_pairs={{0,8},{8,16},{16,24},{24,0},{1,9},{9,17},{17,25},{25,1},{2,10},{10... | collective-permute-start | bytes 1769480 | tf_op jit(solution)/shard_map/ppermute | solution.py:984
  402.8 10.9 %collective-permute-start.20 = (bf16[96,1472]{1,0:T(8,128)(2,1)}, bf16[96,1472]{1,0:T(8,128)(2,1)S(1)}, u32[]{:S(2)}, u32[]{:S(2)}) collective-permute-start(bf16[96,1472]{1,0:T(8,128)(2,1)} %sum_parts.1.refs_0_), channel_id=1, source_target_pairs={{0,24},{8,0},{16,8},{24,16},{1,25},{9,1},{17,9},{25,17},{2,26},{10... | collective-permute-start | bytes 847880 | tf_op jit(solution)/shard_map/ppermute | solution.py:984
  404.7 26.8 %collective-permute-start.19 = (bf16[96,1472]{1,0:T(8,128)(2,1)}, bf16[96,1472]{1,0:T(8,128)(2,1)S(1)}, u32[]{:S(2)}, u32[]{:S(2)}) collective-permute-start(bf16[96,1472]{1,0:T(8,128)(2,1)} %sum_parts.1.refs_0_), channel_id=1, source_target_pairs={{0,16},{8,24},{16,0},{24,8},{1,17},{9,25},{17,1},{25,9},{2,18},{10... | collective-permute-start | bytes 847880 | tf_op jit(solution)/shard_map/ppermute | solution.py:984
  405.8 25.7 %collective-permute-start.18 = (bf16[96,1472]{1,0:T(8,128)(2,1)}, bf16[96,1472]{1,0:T(8,128)(2,1)S(1)}, u32[]{:S(2)}, u32[]{:S(2)}) collective-permute-start(bf16[96,1472]{1,0:T(8,128)(2,1)} %sum_parts.1.refs_0_), channel_id=1, source_target_pairs={{0,8},{8,16},{16,24},{24,0},{1,9},{9,17},{17,25},{25,1},{2,10},{10... | collective-permute-start | bytes 847880 | tf_op jit(solution)/shard_map/ppermute | solution.py:984
  413.7 17.8 %copy-start.19 = (bf16[96,1472]{1,0:T(8,128)(2,1)}, bf16[96,1472]{1,0:T(8,128)(2,1)S(1)}, u32[]{:S(2)}) copy-start(bf16[96,1472]{1,0:T(8,128)(2,1)S(1)} %collective-permute-done.20.refs_3_) | copy-start | bytes 847876
  436.2 26.9 %collective-permute-start.23 = (bf16[96,3200]{1,0:T(8,128)(2,1)}, bf16[96,3200]{1,0:T(8,128)(2,1)S(1)}, u32[]{:S(2)}, u32[]{:S(2)}) collective-permute-start(bf16[96,3200]{1,0:T(8,128)(2,1)} %get-tuple-element.133), channel_id=1, source_target_pairs={{0,6},{1,7},{2,4},{3,5},{4,2},{5,3},{6,0},{7,1},{8,14},{9,15},{10,... | collective-permute-start | bytes 1843208 | tf_op jit(solution)/shard_map/ppermute | solution.py:1156
  438.7 26.2 %collective-permute-start.22 = (bf16[96,3200]{1,0:T(8,128)(2,1)}, bf16[96,3200]{1,0:T(8,128)(2,1)S(1)}, u32[]{:S(2)}, u32[]{:S(2)}) collective-permute-start(bf16[96,3200]{1,0:T(8,128)(2,1)} %get-tuple-element.133), channel_id=1, source_target_pairs={{0,4},{1,5},{2,6},{3,7},{4,0},{5,1},{6,2},{7,3},{8,12},{9,13},{10,... | collective-permute-start | bytes 1843208 | tf_op jit(solution)/shard_map/ppermute | solution.py:1156
  439.3 25.7 %collective-permute-start.21 = (bf16[96,3200]{1,0:T(8,128)(2,1)}, bf16[96,3200]{1,0:T(8,128)(2,1)S(1)}, u32[]{:S(2)}, u32[]{:S(2)}) collective-permute-start(bf16[96,3200]{1,0:T(8,128)(2,1)} %get-tuple-element.133), channel_id=1, source_target_pairs={{0,2},{1,3},{2,0},{3,1},{4,6},{5,7},{6,4},{7,5},{8,10},{9,11},{10,... | collective-permute-start | bytes 1843208 | tf_op jit(solution)/shard_map/ppermute | solution.py:1156
  466.4 4.8 copy-start.3
  466.4 26.0 %copy-start.13 = (f32[768]{0:T(1024)S(1)}, f32[768]{0:T(1024)}, u32[]{:S(2)}) copy-start(f32[768]{0:T(1024)} %param.17) | copy-start | bytes 9220
  466.4 4.7 collective-permute-start.24
  471.2 1.4 copy-start.16
  (7 other events, 7.2 us)
